TPU v7x, 32 devices: a whole 2x2x4 slice. The times are simulated.
32 devices in a mesh: section: 2 (over x), dp: 16 (over z, y, core).
Axes of the slice: x: 2, y: 2, z: 4, core: 2. Of those that a mesh axis runs over, the one named last changes fastest.
Arguments:
- token_ids: int32 [2, 2, 256, 12], P('section', None, 'dp'), may hold values from 0 to 7679
- resets: int32 [2, 2, 256, 12], P('section', None, 'dp'), may hold values 0 or 1
- targets: int32 [2, 256, 12], P(None, 'dp'), may hold values from 0 to 7679
- embedding: bfloat16 [2, 7680, 620], P('section', 'dp'), may hold values from -6 to 6
- input_gates: bfloat16 [2, 3072, 620], P('section', 'dp'), may hold values from -0.25 to 0.25
- recur_gates: bfloat16 [2, 1024, 3072], P('section', 'dp'), may hold values from -0.1875 to 0.1875
- square: bfloat16 [2, 1024, 1024], P('section', 'dp'), may hold values from -0.1875 to 0.1875
- context_gates: bfloat16 [1024, 3072], P(('section', 'dp')), may hold values from -0.1875 to 0.1875
- deep_embed: bfloat16 [1024, 620], P(('section', 'dp')), may hold values from -0.25 to 0.25
- deep_context: bfloat16 [1024, 1024], P(('section', 'dp')), may hold values from -0.1875 to 0.1875
- softmax_weight: bfloat16 [7680, 512], P(('section', 'dp')), may hold values from -0.25 to 0.25
Outputs:
- total_loss: float32 [], replicated
- embedding_grad: float32 [2, 7680, 620], P('section', 'dp')
- input_gates_grad: float32 [2, 3072, 620], P('section', 'dp')
- recur_gates_grad: float32 [2, 1024, 3072], P('section', 'dp')
- square_grad: float32 [2, 1024, 1024], P('section', 'dp')
- context_gates_grad: float32 [1024, 3072], P(('section', 'dp'))
- deep_embed_grad: float32 [1024, 620], P(('section', 'dp'))
- deep_context_grad: float32 [1024, 1024], P(('section', 'dp'))
- softmax_weight_grad: float32 [7680, 512], P(('section', 'dp'))
All inputs are finite; a program needn't handle non-finite values. No bound on the sum of `resets` on one device may be relied on, other than what follows from the above.
Results may differ from a plain program's by a relative error of at most 0.0055.
Values may be sent and summed in bfloat16 or wider, within the bound.
A program may use at most 320 MiB of HBM per device.

v0:
```python
import jax
import jax.numpy as jnp
from jax import lax
from jax.sharding import PartitionSpec as P


def as_sent(x):

    def short(part):
        return part.astype(jnp.bfloat16) if part.dtype == jnp.float32 else part

    return jax.tree.map(short, x)


def shifted(block, axis, distance):
    devices = range(lax.axis_size(axis))
    route = [(i - distance, i) for i in devices if i - distance in devices]
    return lax.ppermute(block, axis, route)


def product(first_mat, second_mat):
    return jnp.dot(first_mat, second_mat, preferred_element_type=jnp.float32)


def outer_sum(first_mat, second_mat):
    return lax.dot_general(
        first_mat, second_mat, (((0,), (0,)), ((), ())), preferred_element_type=jnp.float32
    )


def back_product(first_mat, second_mat):
    return lax.dot_general(
        first_mat, second_mat, (((1,), (1,)), ((), ())), preferred_element_type=jnp.float32
    )


def only_when(condition, function):

    def blank_out():
        return jax.tree.map(jnp.zeros_like, function())

    return lax.cond(condition, function, blank_out)


def gru_forward(inputs, keep_mask, input_weight, recur_weight, context):
    step_count, row_count, in_width = inputs.shape
    hidden = recur_weight.shape[0]
    input_drive = back_product(
        inputs.reshape(step_count * row_count, in_width), input_weight
    ).reshape(step_count, row_count, 3 * hidden)

    def advance(current, step_input):
        drive_now, keep_now = step_input
        before = current * keep_now[:, None]
        before_low = before.astype(jnp.bfloat16)
        recurrent = product(before_low, recur_weight)
        update = jax.nn.sigmoid(drive_now[:, :hidden] + recurrent[:, :hidden] + context[:, :hidden])
        reset_gate = jax.nn.sigmoid(
            drive_now[:, hidden : 2 * hidden]
            + recurrent[:, hidden : 2 * hidden]
            + context[:, hidden : 2 * hidden]
        )
        memory = recurrent[:, 2 * hidden :] + context[:, 2 * hidden :]
        candidate = jnp.tanh(drive_now[:, 2 * hidden :] + reset_gate * memory)
        current = update * before + (1.0 - update) * candidate
        return (current, (current, before_low, before, update, reset_gate, candidate, memory))

    return lax.scan(advance, jnp.zeros((row_count, hidden), jnp.float32), (input_drive, keep_mask))


def gru_grads(flat_input, stored, keep_mask, input_weight, recur_weight, grad_states, grad_last):
    hidden = recur_weight.shape[0]
    before_low = stored[1]

    def retreat(carried, step_input):
        grad_now, keep_now, before_now, update_now, reset_now, cand_now, memory_now = step_input
        total_grad = grad_now + carried
        pre_cand = total_grad * (1.0 - update_now) * (1.0 - cand_now * cand_now)
        pre_update = total_grad * (before_now - cand_now) * update_now * (1.0 - update_now)
        pre_reset = pre_cand * memory_now * reset_now * (1.0 - reset_now)
        recur_grad = jnp.concatenate([pre_update, pre_reset, pre_cand * reset_now], axis=1)
        recur_low = recur_grad.astype(jnp.bfloat16)
        drive_grad = jnp.concatenate([pre_update, pre_reset, pre_cand], axis=1)
        carried = (total_grad * update_now + back_product(recur_low, recur_weight)) * keep_now[
            :, None
        ]
        return (carried, (drive_grad, recur_grad, recur_low))

    _, (drive_grad, recur_grad, recur_low) = lax.scan(
        retreat,
        grad_last,
        (grad_states, keep_mask, stored[2], stored[3], stored[4], stored[5], stored[6]),
        reverse=True,
    )
    grad_recur_weight = outer_sum(before_low.reshape(-1, hidden), recur_low.reshape(-1, 3 * hidden))
    drive_low = drive_grad.reshape(-1, 3 * hidden).astype(jnp.bfloat16)
    grad_input_weight = outer_sum(drive_low, flat_input)
    input_grad = product(drive_low, input_weight)
    return (grad_input_weight, grad_recur_weight, input_grad, jnp.sum(recur_grad, axis=0))


def per_device(
    token_ids,
    resets,
    targets,
    embedding,
    input_gates,
    recur_gates,
    square,
    context_gates,
    deep_embed,
    deep_context,
    softmax_weight,
):
    embed_full, input_full, recur_full, square_full = (
        lax.all_gather(embedding[0], "dp", axis=0, tiled=True),
        lax.all_gather(input_gates[0], "dp", axis=0, tiled=True),
        lax.all_gather(recur_gates[0], "dp", axis=0, tiled=True),
        lax.all_gather(square[0], "dp", axis=0, tiled=True),
    )
    gates_full, embed_deep, context_deep, output_full = (
        lax.all_gather(context_gates, ("section", "dp"), axis=0, tiled=True),
        lax.all_gather(deep_embed, ("section", "dp"), axis=0, tiled=True),
        lax.all_gather(deep_context, ("section", "dp"), axis=0, tiled=True),
        lax.all_gather(softmax_weight, ("section", "dp"), axis=0, tiled=True),
    )
    section_index = lax.axis_index("section")
    is_decoder = section_index == 1
    is_encoder = section_index == 0
    micro_count = token_ids.shape[1]
    row_count = token_ids.shape[2]
    step_count = token_ids.shape[3]
    hidden = recur_full.shape[0]
    vocab_size = embed_full.shape[0]
    unit_count = output_full.shape[1]
    token_count = step_count * row_count
    loss_scale = 1.0 / (micro_count * row_count * lax.axis_size("dp"))
    token_rows = jnp.transpose(token_ids[0], (0, 2, 1))
    keep_mask = jnp.transpose(1 - resets[0], (0, 2, 1)).astype(jnp.float32)
    labels = jnp.transpose(targets, (0, 2, 1)).reshape(-1)
    no_context = jnp.zeros((row_count, 3 * hidden), jnp.float32)
    embedded = [
        jnp.take(embed_full, token_rows[batch_index], axis=0) for batch_index in range(micro_count)
    ]

    def encode_all():
        contexts, records = ([], [])
        for batch_index in range(micro_count):
            last_state, stored = gru_forward(
                embedded[batch_index], keep_mask[batch_index], input_full, recur_full, no_context
            )
            last_low = last_state.astype(jnp.bfloat16)
            context_tanh = jnp.tanh(product(last_low, square_full))
            contexts.append(context_tanh.astype(jnp.bfloat16))
            records.append((stored, last_low, context_tanh))
        return (jnp.stack(contexts), records)

    contexts, enc_records = only_when(is_encoder, encode_all)
    context_in = jax.tree.map(
        lambda part, own: part.astype(own.dtype), shifted(as_sent(contexts), "section", 1), contexts
    )

    def decode_all():
        records, smooth_rows = ([], [])
        for batch_index in range(micro_count):
            context = context_in[batch_index]
            inputs = embedded[batch_index]
            _, stored = gru_forward(
                inputs, keep_mask[batch_index], input_full, recur_full, product(context, gates_full)
            )
            states_low = stored[0].reshape(token_count, hidden).astype(jnp.bfloat16)
            deep_pre = product(states_low, square_full) + back_product(
                inputs.reshape(token_count, -1), embed_deep
            )
            deep_pre = (
                deep_pre.reshape(step_count, row_count, -1) + product(context, context_deep)[None]
            ).reshape(token_count, -1)
            smooth = jnp.logaddexp(deep_pre[:, :unit_count], deep_pre[:, unit_count:])
            smooth_rows.append(smooth.astype(jnp.bfloat16))
            records.append((stored, states_low, deep_pre, smooth))
        return (records, jnp.concatenate(smooth_rows, axis=0))

    dec_records, smooth_all = only_when(is_decoder, decode_all)

    def head_rows(smooth_in, weight_rows):
        logits = back_product(smooth_in, weight_rows)
        row_max = jnp.max(logits, axis=1)
        row_total = jnp.sum(jnp.exp(logits - row_max[:, None]), axis=1)
        target_hit = lax.broadcasted_iota(jnp.int32, logits.shape, 1) == labels[:, None]
        picked = jnp.sum(jnp.where(target_hit, logits, 0.0), axis=1)
        return (logits, target_hit, row_max, row_total, picked)

    def logit_grads(logits, target_hit, log_norm):
        return (
            (jnp.exp(logits - log_norm[:, None]) - target_hit.astype(jnp.float32)) * loss_scale
        ).astype(jnp.bfloat16)

    def head_whole():
        logits, target_hit, row_max, row_total, picked = head_rows(smooth_all, output_full)
        log_norm = row_max + jnp.log(row_total)
        logit_low = logit_grads(logits, target_hit, log_norm)
        return (
            jnp.sum(log_norm - picked) * loss_scale,
            product(logit_low, output_full),
            outer_sum(logit_low, smooth_all),
        )

    loss_part, smooth_grad, output_grad = only_when(is_decoder, head_whole)

    def decode_back():
        grad_sums = None
        context_grads = []
        for batch_index in range(micro_count):
            stored, states_low, deep_pre, smooth = dec_records[batch_index]
            context = context_in[batch_index]
            flat_input = embedded[batch_index].reshape(token_count, -1)
            smooth_slice = smooth_grad[batch_index * token_count : (batch_index + 1) * token_count]
            deep_grad = jnp.concatenate(
                [
                    smooth_slice * jnp.exp(deep_pre[:, :unit_count] - smooth),
                    smooth_slice * jnp.exp(deep_pre[:, unit_count:] - smooth),
                ],
                axis=1,
            )
            deep_low = deep_grad.astype(jnp.bfloat16)
            state_grad = back_product(deep_low, square_full).reshape(step_count, row_count, hidden)
            outer_low = jnp.sum(deep_grad.reshape(step_count, row_count, -1), axis=0).astype(
                jnp.bfloat16
            )
            grad_input_weight, grad_recur_weight, input_grad, drive_sum = gru_grads(
                flat_input,
                stored,
                keep_mask[batch_index],
                input_full,
                recur_full,
                state_grad,
                jnp.zeros((row_count, hidden), jnp.float32),
            )
            input_grad = input_grad + product(deep_low, embed_deep)
            drive_sum_low = drive_sum.astype(jnp.bfloat16)
            context_grad = back_product(outer_low, context_deep) + back_product(
                drive_sum_low, gates_full
            )
            context_grads.append(context_grad.astype(jnp.bfloat16))
            term_list = (
                jax.ops.segment_sum(input_grad, token_rows[batch_index].reshape(-1), vocab_size),
                grad_input_weight,
                grad_recur_weight,
                outer_sum(states_low, deep_low),
                outer_sum(context, drive_sum_low),
                outer_sum(deep_low, flat_input),
                outer_sum(context, outer_low),
            )
            grad_sums = (
                term_list if grad_sums is None else jax.tree.map(jnp.add, grad_sums, term_list)
            )
        return (jnp.stack(context_grads), grad_sums[:4], grad_sums[4:])

    context_low, dec_terms, only_terms = only_when(is_decoder, decode_back)
    context_back = shifted(as_sent(context_low), "section", -1).astype(context_low.dtype)

    def encode_back():
        grad_sums = None
        for batch_index in range(micro_count):
            stored, last_low, context_tanh = enc_records[batch_index]
            flat_input = embedded[batch_index].reshape(token_count, -1)
            pre_low = (
                context_back[batch_index].astype(jnp.float32) * (1.0 - context_tanh * context_tanh)
            ).astype(jnp.bfloat16)
            grad_input_weight, grad_recur_weight, input_grad, _ = gru_grads(
                flat_input,
                stored,
                keep_mask[batch_index],
                input_full,
                recur_full,
                jnp.zeros((step_count, row_count, hidden), jnp.float32),
                back_product(pre_low, square_full),
            )
            term_list = (
                jax.ops.segment_sum(input_grad, token_rows[batch_index].reshape(-1), vocab_size),
                grad_input_weight,
                grad_recur_weight,
                outer_sum(last_low, pre_low),
            )
            grad_sums = (
                term_list if grad_sums is None else jax.tree.map(jnp.add, grad_sums, term_list)
            )
        return grad_sums

    half_terms = lax.cond(is_encoder, encode_back, lambda: dec_terms)
    table_grad, input_grad_w, recur_grad_w, square_grad = (
        lax.psum_scatter(half_terms[0], "dp", scatter_dimension=0, tiled=True),
        lax.psum_scatter(half_terms[1], "dp", scatter_dimension=0, tiled=True),
        lax.psum_scatter(half_terms[2], "dp", scatter_dimension=0, tiled=True),
        lax.psum_scatter(half_terms[3], "dp", scatter_dimension=0, tiled=True),
    )
    gates_grad, embed_grad, context_grad_w, softmax_grad = (
        lax.psum_scatter(only_terms[0], ("section", "dp"), scatter_dimension=0, tiled=True),
        lax.psum_scatter(only_terms[1], ("section", "dp"), scatter_dimension=0, tiled=True),
        lax.psum_scatter(only_terms[2], ("section", "dp"), scatter_dimension=0, tiled=True),
        lax.psum_scatter(output_grad, ("section", "dp"), scatter_dimension=0, tiled=True),
    )
    total_loss = lax.psum(loss_part, ("section", "dp"))
    return (
        total_loss,
        table_grad[None],
        input_grad_w[None],
        recur_grad_w[None],
        square_grad[None],
        gates_grad,
        embed_grad,
        context_grad_w,
        softmax_grad,
    )


def solution(mesh):
    in_specs = (
        P("section", None, "dp", None),
        P("section", None, "dp", None),
        P(None, "dp", None),
        P("section", "dp", None),
        P("section", "dp", None),
        P("section", "dp", None),
        P("section", "dp", None),
        P(("section", "dp"), None),
        P(("section", "dp"), None),
        P(("section", "dp"), None),
        P(("section", "dp"), None),
    )
    out_specs = (
        P(),
        P("section", "dp", None),
        P("section", "dp", None),
        P("section", "dp", None),
        P("section", "dp", None),
        P(("section", "dp"), None),
        P(("section", "dp"), None),
        P(("section", "dp"), None),
        P(("section", "dp"), None),
    )
    return jax.shard_map(
        per_device, mesh=mesh, in_specs=in_specs, out_specs=out_specs, check_vma=False
    )
```

profile of v0, /device:TPU:0, one launch (start us, length us, event | category | flops | bytes accessed | tf_op | source)
XLA Modules:
  0.0 2255.2 jit_solution(8473314022965684124)
XLA Ops:
  14.3 82.6 %all-gather.21.cloned.1.call-done = bf16[1,7680,620]{2,1,0:T(8,128)(2,1)} async-done(((bf16[1,480,620]{2,1,0:T(8,128)(2,1)}), bf16[1,7680,620]{2,1,0:T(8,128)(2,1)}) %all-gather.21.cloned.1.call-update) | async-done | bytes 9523216 | tf_op jit(solution)/shard_map/all_gather | solution.py:116
  96.9 6.2 gather_fusion.1
  103.1 6.3 gather_fusion
  109.6 29.1 %all-gather.27.cloned.1.call-done = bf16[1,1024,1024]{2,1,0:T(8,128)(2,1)} async-done(((bf16[1,64,1024]{2,1,0:T(8,128)(2,1)}), bf16[1,1024,1024]{2,1,0:T(8,128)(2,1)}) %all-gather.27.cloned.1.call-update) | async-done | bytes 2097168 | tf_op jit(solution)/shard_map/all_gather | solution.py:119
  138.7 49.9 %all-gather.23.cloned.1.call-done = bf16[1,3072,620]{2,1,0:T(8,128)(2,1)} async-done(((bf16[1,192,620]{2,1,0:T(8,128)(2,1)}), bf16[1,3072,620]{2,1,0:T(8,128)(2,1)}) %all-gather.23.cloned.1.call-update) | async-done | bytes 3809296 | tf_op jit(solution)/shard_map/all_gather | solution.py:117
  188.5 63.1 %all-gather.25.cloned.1.call-done = bf16[1,1024,3072]{2,1,0:T(8,128)(2,1)} async-done(((bf16[1,64,3072]{2,1,0:T(8,128)(2,1)}), bf16[1,1024,3072]{2,1,0:T(8,128)(2,1)}) %all-gather.25.cloned.1.call-update) | async-done | bytes 6291472 | tf_op jit(solution)/shard_map/all_gather | solution.py:118
  251.6 184.4 %conditional.5 = (bf16[2,16,1024]{2,1,0:T(8,128)(2,1)}, bf16[12,16,1024]{2,1,0:T(8,128)(2,1)}, f32[12,16,1024]{2,1,0:T(8,128)}, f32[12,16,1024]{2,1,0:T(8,128)},...) conditional(s32[]{:T(128)} %convert_element_type.224, ...), branch_computations={%region_0.0_spmd, %region_1.7_spmd} | conditional | flops 1732411392 | bytes 69867496 | solution.py:42
  252.3 5.2 fusion.56
  265.1 75.2 %while.168 = (s32[]{:T(128)}, f32[16,1024]{1,0:T(8,128)S(1)}, bf16[12,16,1024]{2,1,0:T(8,128)(2,1)}, f32[12,16,1024]{2,1,0:T(8,128)}, f32[12,16,1024]{2,1,0:T(8,...) while((s32[]{:T(128)}, f32[16,1024]{1,0:T(8,128)S(1)}, ...), condition=%wide.region_3.4_spmd.clone, body=%wide.region_2.3_spmd.clone.sunk | while | flops 101220352 | bytes 8356834 | solution.py:68
  346.1 83.6 %while.169 = (s32[]{:T(128)}, f32[16,1024]{1,0:T(8,128)S(1)}, bf16[12,16,1024]{2,1,0:T(8,128)(2,1)}, f32[12,16,1024]{2,1,0:T(8,128)}, f32[12,16,1024]{2,1,0:T(8,...) while((s32[]{:T(128)}, f32[16,1024]{1,0:T(8,128)S(1)}, ...), condition=%wide.region_5.6_spmd.clone, body=%wide.region_4.5_spmd.clone.sunk | while | flops 101220352 | bytes 8356386 | solution.py:68
  440.3 16.7 conditional.6
  457.0 56.7 %all-gather.19.cloned.1.call-done = bf16[7680,512]{1,0:T(8,128)(2,1)} async-done(((bf16[240,512]{1,0:T(8,128)(2,1)}), bf16[7680,512]{1,0:T(8,128)(2,1)}) %all-gather.19.cloned.1.call-update) | async-done | bytes 7864336 | tf_op jit(solution)/shard_map/all_gather | solution.py:125
  516.2 5.4 copy-done.8
  521.7 36.3 %conditional.8 = (bf16[2,16,1024]{2,1,0:T(8,128)(2,1)}, f32[7680,620]{1,0:T(8,128)}, f32[3072,620]{0,1:T(8,128)}, f32[1024,3072]{0,1:T(8,128)}, f32[1024,1024]{0...) conditional(s32[]{:T(128)} %convert_element_type.220, () %tuple.150, ...), branch_computations={%region_19.21_spmd, %region_20.31_spmd} | conditional | flops 8684677120 | bytes 302558080 | solution.py:42
  533.4 6.1 broadcast.171.clone
  539.5 6.1 broadcast.171
  545.6 7.8 broadcast.169
  562.6 472.7 %collective-permute-done.1 = bf16[2,16,1024]{2,1,0:T(8,128)(2,1)S(1)} collective-permute-done((bf16[2,16,1024]{2,1,0:T(8,128)(2,1)}, bf16[2,16,1024]{2,1,0:T(8,128)(2,1)S(1)}, u32[]{:S(2)}, u32[]{:S(2)}) %collective-permute-start.1) | collective-permute-done | bytes 65568 | tf_op jit(solution)/shard_map/ppermute | solution.py:18
  1035.4 214.1 %conditional.9 = ((f32[7680,620]{1,0:T(8,128)}, f32[3072,620]{0,1:T(8,128)}, f32[1024,3072]{0,1:T(8,128)}, f32[1024,1024]{0,1:T(8,128)})) conditional(s32[]{:T(128)} %convert_element_type.224, (f32[7680,620]{1,0:T(8,128)}, f32[3072,620]{0,1:T(8,128)}, f32[1024,3072]{0,1:T(8,128)}, f32[1024,1024]{0,1:T(8,128)}) %tuple.152, ...), branch_computations={%region_30.32_spmd, %region_31.38_spmd} | conditional | flops 5686318592 | bytes 147959872 | solution.py:290
  1039.9 84.9 %while.167 = (s32[]{:T(128)}, f32[16,1024]{1,0:T(8,128)S(1)}, bf16[12,16,3072]{2,1,0:T(8,128)(2,1)S(1)}, bf16[12,16,3072]{2,1,0:T(8,128)(2,1)}, f32[12,16,1024]{...) while((s32[]{:T(128)}, f32[16,1024]{1,0:T(8,128)S(1)}, ...), condition=%wide.region_35.36_spmd, body=%wide.region_34.35_spmd.sunk | while | flops 101875712 | bytes 7700829 | solution.py:89
  1041.8 4.6 fusion.348
  1048.9 4.5 fusion.348
  1056.0 4.5 fusion.348
  1063.0 4.5 fusion.348
  1077.1 4.5 fusion.348
  1084.2 4.6 fusion.348
  1091.3 4.6 fusion.348
  1098.4 4.5 fusion.348
  1105.5 4.5 fusion.348
  1129.3 84.9 %while.166 = (s32[]{:T(128)}, f32[16,1024]{1,0:T(8,128)S(1)}, bf16[12,16,3072]{2,1,0:T(8,128)(2,1)S(1)}, bf16[12,16,3072]{2,1,0:T(8,128)(2,1)}, f32[12,16,1024]{...) while((s32[]{:T(128)}, f32[16,1024]{1,0:T(8,128)S(1)}, ...), condition=%wide.region_33.34_spmd, body=%wide.region_32.33_spmd.sunk | while | flops 101875712 | bytes 7700829 | solution.py:89
  1131.2 4.5 fusion.341
  1152.4 4.5 fusion.341
  1159.4 4.5 fusion.341
  1166.5 4.5 fusion.341
  1231.9 6.4 fusion.126
  1238.2 10.9 scatter_custom_fusion.1
  1249.5 5.3 copy.36
  1254.9 5.4 copy.39
  1260.4 9.3 copy.34
  1269.7 12.8 copy.37
  1282.6 12.7 copy.35
  1296.4 40.4 %psum.7 = f32[]{:T(128)} all-reduce(f32[]{:T(128)} %get-tuple-element.1512), channel_id=1, replica_groups=mesh['section'=2,'dp'=16] {'section','dp'}, use_global_device_ids=true, to_apply=%region_18.20 | all-reduce | flops 1 | bytes 8 | tf_op jit(solution)/shard_map/psum | solution.py:303
  1336.8 132.4 %reduce-scatter.21.cloned.1.call-done = f32[32,1024]{1,0:T(8,128)} async-done(((f32[1024,1024]{1,0:T(8,128)}), f32[32,1024]{1,0:T(8,128)}) %reduce-scatter.21.cloned.1.call-update) | async-done | bytes 131088 | tf_op jit(solution)/shard_map/reduce_scatter | solution.py:300
  1469.2 97.0 %reduce-scatter.11.cloned.1.call-done = f32[192,620]{1,0:T(8,128)} async-done(((f32[3072,620]{1,0:T(8,128)}), f32[192,620]{1,0:T(8,128)}) %reduce-scatter.11.cloned.1.call-update) | async-done | bytes 476176 | tf_op jit(solution)/shard_map/reduce_scatter | solution.py:293
  1566.2 163.0 %reduce-scatter.17.cloned.1.call-done = f32[32,3072]{1,0:T(8,128)} async-done(((f32[1024,3072]{1,0:T(8,128)}), f32[32,3072]{1,0:T(8,128)}) %reduce-scatter.17.cloned.1.call-update) | async-done | bytes 393232 | tf_op jit(solution)/shard_map/reduce_scatter | solution.py:298
  1729.2 138.3 %reduce-scatter.13.cloned.1.call-done = f32[64,3072]{1,0:T(8,128)} async-done(((f32[1024,3072]{1,0:T(8,128)}), f32[64,3072]{1,0:T(8,128)}) %reduce-scatter.13.cloned.1.call-update) | async-done | bytes 786448 | tf_op jit(solution)/shard_map/reduce_scatter | solution.py:294
  1867.6 176.3 %reduce-scatter.23.cloned.1.call-done = f32[240,512]{1,0:T(8,128)} async-done(((f32[7680,512]{1,0:T(8,128)}), f32[240,512]{1,0:T(8,128)}) %reduce-scatter.23.cloned.1.call-update) | async-done | bytes 491536 | tf_op jit(solution)/shard_map/reduce_scatter | solution.py:301
  2043.8 204.3 %reduce-scatter.9.cloned.1.call-done = f32[480,620]{1,0:T(8,128)} async-done(((f32[7680,620]{1,0:T(8,128)}), f32[480,620]{1,0:T(8,128)}) %reduce-scatter.9.cloned.1.call-update) | async-done | bytes 1190416 | tf_op jit(solution)/shard_map/reduce_scatter | solution.py:292
  (400 shorter events, 365.7 us)
Async XLA Ops:
  7.2 89.7 %all-gather.21.cloned.1.call-start = ((), (), s32[]{:S(2)}) async-start(), calls=%async_computation.20 | async-start | bytes 10444800 | tf_op jit(solution)/shard_map/all_gather | solution.py:116
  7.9 130.7 %all-gather.27.cloned.1.call-start = ((), (), s32[]{:S(2)}) async-start(), calls=%async_computation.23 | async-start | bytes 2228224 | tf_op jit(solution)/shard_map/all_gather | solution.py:119
  8.7 179.9 %all-gather.23.cloned.1.call-start = ((), (), s32[]{:S(2)}) async-start(), calls=%async_computation.21 | async-start | bytes 4177920 | tf_op jit(solution)/shard_map/all_gather | solution.py:117
  9.4 242.3 %all-gather.25.cloned.1.call-start = ((), (), s32[]{:S(2)}) async-start(), calls=%async_computation.22 | async-start | bytes 6684672 | tf_op jit(solution)/shard_map/all_gather | solution.py:118
  10.0 428.0 %all-gather.15.cloned.1.call-start = ((), (), s32[]{:S(2)}) async-start(), calls=%async_computation.9 | async-start | bytes 1351680 | tf_op jit(solution)/shard_map/all_gather | solution.py:123
  10.6 427.4 %all-gather.17.cloned.1.call-start = ((), (), s32[]{:S(2)}) async-start(), calls=%async_computation.10 | async-start | bytes 2162688 | tf_op jit(solution)/shard_map/all_gather | solution.py:124
  11.1 426.8 %all-gather.13.cloned.1.call-start = ((), (), s32[]{:S(2)}) async-start(), calls=%async_computation.8 | async-start | bytes 6488064 | tf_op jit(solution)/shard_map/all_gather | solution.py:122
  11.9 501.8 %all-gather.19.cloned.1.call-start = ((), (), s32[]{:S(2)}) async-start(), calls=%async_computation.11 | async-start | bytes 8110080 | tf_op jit(solution)/shard_map/all_gather | solution.py:125
  12.6 1324.2 %reduce-scatter.19.cloned.1.call-start = ((), (), s32[]{:S(2)}) async-start(), calls=%async_computation.17 | async-start | bytes 2703360 | tf_op jit(solution)/shard_map/reduce_scatter | solution.py:299
  109.5 330.1 %copy-start.13 = (bf16[12,16,620]{2,1,0:T(8,128)(2,1)}, bf16[12,16,620]{2,1,0:T(8,128)(2,1)S(1)}, u32[]{:S(2)}) copy-start(bf16[12,16,620]{2,1,0:T(8,128)(2,1)S(1)} %get-tuple-element.2125) | copy-start | bytes 714244
  109.5 330.1 %copy-start.17 = (bf16[12,16,620]{2,1,0:T(8,128)(2,1)}, bf16[12,16,620]{2,1,0:T(8,128)(2,1)S(1)}, u32[]{:S(2)}) copy-start(bf16[12,16,620]{2,1,0:T(8,128)(2,1)S(1)} %get-tuple-element.2126) | copy-start | bytes 714244
  251.6 185.7 %copy-start.53 = (s32[2,16,12]{1,0,2:T(2,128)S(1)}, s32[2,16,12]{1,0,2:T(2,128)}, u32[]{:S(2)}) copy-start(s32[2,16,12]{1,0,2:T(2,128)} %param.41) | copy-start | bytes 4612
  252.2 5.2 copy-start
  340.3 5.7 copy-start.35
  346.1 84.8 %copy-start.4 = (bf16[1024,1024]{1,0:T(8,128)(2,1)S(1)}, bf16[1024,1024]{1,0:T(8,128)(2,1)}, u32[]{:S(2)}) copy-start(bf16[1024,1024]{1,0:T(8,128)(2,1)} %get-tuple-element.1264) | copy-start | bytes 6291460 | tf_op jit(solution)/shard_map/cond
  436.0 3.6 collective-permute-start
  439.6 0.6 copy-start.44
  457.0 56.7 %copy-start.32 = (f32[12,16,1024]{2,1,0:T(8,128)}, f32[12,16,1024]{2,1,0:T(8,128)S(1)}, u32[]{:S(2)}) copy-start(f32[12,16,1024]{2,1,0:T(8,128)S(1)} %get-tuple-element.1516) | copy-start | bytes 2359300
  513.7 2.5 copy-start.3
  513.7 2.5 copy-start.14
  516.2 5.5 copy-start.8
  558.0 477.4 %copy-start.18 = (bf16[12,16,620]{2,1,0:T(8,128)(2,1)S(1)}, bf16[12,16,620]{2,1,0:T(8,128)(2,1)}, u32[]{:S(2)}) copy-start(bf16[12,16,620]{2,1,0:T(8,128)(2,1)} %copy-done.17) | copy-start | bytes 714244
  561.3 775.5 %reduce-scatter.15.cloned.1.call-start = ((), (), s32[]{:S(2)}) async-start(), calls=%async_computation.15 | async-start | bytes 4456448 | tf_op jit(solution)/shard_map/reduce_scatter | solution.py:295
  561.3 474.0 %collective-permute-start.1 = (bf16[2,16,1024]{2,1,0:T(8,128)(2,1)}, bf16[2,16,1024]{2,1,0:T(8,128)(2,1)S(1)}, u32[]{:S(2)}, u32[]{:S(2)}) collective-permute-start(bf16[2,16,1024]{2,1,0:T(8,128)(2,1)} %get-tuple-element.1536), channel_id=1, source_target_pairs={{16,0},{17,1},{18,2},{19,3},{20,4},{21,5},{22,6},{23,7},{24,8},{25... | collective-permute-start | bytes 196616 | tf_op jit(solution)/shard_map/ppermute | solution.py:18
  1224.6 4.3 copy-start.41
  1228.9 3.0 copy-start.42
  1228.9 3.0 copy-start.47
  1231.9 6.4 copy-start.38
  1254.8 214.4 %reduce-scatter.21.cloned.1.call-start = ((), (), s32[]{:S(2)}) async-start(), calls=%async_computation.18 | async-start | bytes 4325376 | tf_op jit(solution)/shard_map/reduce_scatter | solution.py:300
  1260.3 305.9 %reduce-scatter.11.cloned.1.call-start = ((), (), s32[]{:S(2)}) async-start(), calls=%async_computation.13 | async-start | bytes 8355840 | tf_op jit(solution)/shard_map/reduce_scatter | solution.py:293
  1269.7 459.6 %reduce-scatter.17.cloned.1.call-start = ((), (), s32[]{:S(2)}) async-start(), calls=%async_computation.16 | async-start | bytes 12976128 | tf_op jit(solution)/shard_map/reduce_scatter | solution.py:298
  1282.5 585.0 %reduce-scatter.13.cloned.1.call-start = ((), (), s32[]{:S(2)}) async-start(), calls=%async_computation.14 | async-start | bytes 13369344 | tf_op jit(solution)/shard_map/reduce_scatter | solution.py:294
  1295.3 748.5 %reduce-scatter.23.cloned.1.call-start = ((), (), s32[]{:S(2)}) async-start(), calls=%async_computation.19 | async-start | bytes 16220160 | tf_op jit(solution)/shard_map/reduce_scatter | solution.py:301
  1295.9 952.3 %reduce-scatter.9.cloned.1.call-start = ((), (), s32[]{:S(2)}) async-start(), calls=%async_computation.12 | async-start | bytes 20889600 | tf_op jit(solution)/shard_map/reduce_scatter | solution.py:292
Sparse Core Ops, SparseCore 0:
  10.3 86.5 all-gather.20
  99.0 39.5 all-gather.26
  140.9 47.5 all-gather.22
  190.7 60.9 all-gather.24
  254.3 52.9 all-gather.14
  310.0 55.4 all-gather.16
  368.4 68.4 all-gather.12
  439.8 73.8 all-gather.18
  561.4 605.2 reduce-scatter.18
  1255.0 71.1 reduce-scatter.14
  1329.1 140.0 reduce-scatter.20
  1474.2 91.9 reduce-scatter.10
  1573.9 155.3 reduce-scatter.16
  1733.7 133.8 reduce-scatter.12
  1874.0 169.7 reduce-scatter.22
  2048.4 199.6 reduce-scatter.8
where the time goes:
time: 2270 us; the launch traced here: 2260 us
  waiting for transfers between devices  1670 us (74%)
  matrix products  241 us (11%)
  local copies, waits for them, and re-layouts  164 us (7%)
  other arithmetic  112 us (5%)
  blocking collectives  40.4 us (2%)
    ppermute x2, waiting for transfers between devices, shifted(): return lax.ppermute(block, axis, route)  474 us
    reduce_scatter x1, waiting for transfers between devices, per_device(): lax.psum_scatter(half_terms[0], 'dp', scatter_dimension=0, tiled=True)  204 us
    reduce_scatter x1, waiting for transfers between devices, per_device(): lax.psum_scatter(output_grad, ('section', 'dp'), scatter_dimension=0, til...  176 us
    reduce_scatter x1, waiting for transfers between devices, per_device(): lax.psum_scatter(only_terms[0], ('section', 'dp'), scatter_dimension=0, t...  163 us
    reduce_scatter x1, waiting for transfers between devices, per_device(): lax.psum_scatter(half_terms[2], 'dp', scatter_dimension=0, tiled=True)  138 us
    reduce_scatter x1, waiting for transfers between devices, per_device(): lax.psum_scatter(only_terms[2], ('section', 'dp'), scatter_dimension=0, t...  132 us
    dot_general x28, matrix products, back_product(): lax.dot_general(first_mat, second_mat, (((1,), (1,)), ((), ())), preferre...  120 us
    dot_general x28, matrix products, product(): return jnp.dot(first_mat, second_mat, preferred_element_type=jnp.float32)  101 us
  transfers between devices with their start and end apart: 18, of which 13 were waited for; matrix products, arithmetic and copies ran while one was open for 21% of the time, Pallas kernels for 0%

commit v1 on v0

v1 whole, which is shorter than its diff:
```python
import functools

import jax
import jax.numpy as jnp
from jax import lax
from jax.experimental import pallas as pl
from jax.experimental.pallas import tpu as pltpu
from jax.sharding import PartitionSpec as P

MESH = pl.DeviceIdType.MESH
ANY = pl.BlockSpec(memory_space=pl.ANY)
VMEM = pl.BlockSpec(memory_space=pltpu.VMEM)
f32 = jnp.float32
bf16 = jnp.bfloat16
VMEM_LIMIT = 60 * 2**20


def nn(a, b):
    return jnp.dot(a, b, preferred_element_type=f32)


def nt(a, b):
    return lax.dot_general(a, b, (((1,), (1,)), ((), ())), preferred_element_type=f32)


def tn(a, b):
    return lax.dot_general(a, b, (((0,), (0,)), ((), ())), preferred_element_type=f32)


def factors(n):
    z = 4 if n % 8 == 0 else 1
    return z, n // (2 * z)


class Place:
    def __init__(self, n):
        self.Z, self.Y = factors(n)
        self.s = lax.axis_index("section")
        d = lax.axis_index("dp")
        self.d = d
        self.c = d % 2
        self.zy = d // 2
        self.y = self.zy % self.Y
        self.z = self.zy // self.Y

    def along_z(self, step):
        return lax.rem(self.z + step + self.Z, self.Z)

    def along_y(self, step):
        return lax.rem(self.y + step + self.Y, self.Y)

    def device(self, z, y, c):
        return (self.s, (z * self.Y + y) * 2 + c)

    def partners(self):
        found = [self.device(self.along_z(k), self.y, self.c) for k in range(1, self.Z)]
        found += [self.device(self.z, self.along_y(k), self.c) for k in range(1, self.Y)]
        return found + [self.device(self.z, self.y, 1 - self.c), (1 - self.s, self.d)]


def greet(devices):
    barrier = pltpu.get_barrier_semaphore()
    for device in devices:
        pl.semaphore_signal(barrier, inc=1, device_id=device, device_id_type=MESH)
    pl.semaphore_wait(barrier, len(devices))


def remote(src, dst, send, recv, device):
    return pltpu.make_async_remote_copy(
        src_ref=src, dst_ref=dst, send_sem=send, recv_sem=recv, device_id=device, device_id_type=MESH
    )


def arrival(ref, sem):
    return pltpu.make_async_copy(ref, ref, sem)


def gather_kernel(n, crossed, *refs):
    count = len(crossed)
    sources, outs = refs[:count], refs[count : 2 * count]
    z_sem, y_sem, c_sem, s_sem, l_sem, x_sem, xs_sem = refs[2 * count :]
    at = Place(n)
    Z, Y = at.Z, at.Y
    greet(at.partners())

    x_copies = []
    for item in range(count):
        if crossed[item]:
            copy = remote(
                sources[item],
                outs[item].at[at.s, at.zy, at.c],
                xs_sem.at[item],
                x_sem.at[item],
                (1 - at.s, at.d),
            )
            copy.start()
            x_copies.append(copy)

    units = []
    for item in range(count):
        if crossed[item]:
            units.append((item, outs[item].at[at.s], sources[item]))
        else:
            units.append((item, outs[item], sources[item]))
    own = len(units)
    for item in range(count):
        if crossed[item]:
            gathered = outs[item].at[1 - at.s]
            units.append((item, gathered, gathered.at[at.zy, at.c]))

    def spread(u, src, zy, z_slot, to_z, to_y):
        gathered = units[u][1]
        dst = gathered.at[zy, at.c]
        if to_z:
            for k in range(1, Z):
                remote(
                    src, dst, s_sem.at[u], z_sem.at[u, k - 1], at.device(at.along_z(k), at.y, at.c)
                ).start()
        if to_y:
            for k in range(1, Y):
                remote(
                    src,
                    dst,
                    s_sem.at[u],
                    y_sem.at[u, z_slot * (Y - 1) + k - 1],
                    at.device(at.z, at.along_y(k), at.c),
                ).start()
        remote(src, dst, s_sem.at[u], c_sem.at[u], at.device(at.z, at.y, 1 - at.c)).start()

    for u, (item, gathered, src) in enumerate(units):
        if u < own:
            pltpu.make_async_copy(src, gathered.at[at.zy, at.c], l_sem.at[u]).start()
        else:
            arrival(src, x_sem.at[item]).wait()
        spread(u, src, at.zy, 0, True, True)
    for u, (item, gathered, _) in enumerate(units):
        for k in range(1, Z):
            zy = at.along_z(-k) * Y + at.y
            block = gathered.at[zy, at.c]
            arrival(block, z_sem.at[u, k - 1]).wait()
            spread(u, block, zy, k, False, True)
        for slot in range(Z):
            for k in range(1, Y):
                zy = at.along_z(-slot) * Y + at.along_y(-k)
                block = gathered.at[zy, at.c]
                arrival(block, y_sem.at[u, slot * (Y - 1) + k - 1]).wait()
                spread(u, block, zy, 0, False, False)
    for u, (item, gathered, src) in enumerate(units):
        if u < own:
            pltpu.make_async_copy(src, gathered.at[at.zy, at.c], l_sem.at[u]).wait()
        theirs = gathered.at[:, 1 - at.c]
        arrival(theirs, c_sem.at[u]).wait()
        most = gathered.at[pl.ds(0, Z * Y - 1)]
        arrival(most, s_sem.at[u]).wait()
        arrival(gathered.at[0, 0], s_sem.at[u]).wait()
    for copy in x_copies:
        copy.wait_send()


def gather(n, arrays, crossed):
    Z, Y = factors(n)
    shapes = []
    for array, over_section in zip(arrays, crossed):
        lead = (2, Z * Y, 2) if over_section else (Z * Y, 2)
        shapes.append(jax.ShapeDtypeStruct(lead + array.shape, array.dtype))
    units = len(arrays) + sum(crossed)
    dma = pltpu.SemaphoreType.DMA
    return pl.pallas_call(
        functools.partial(gather_kernel, n, crossed),
        out_shape=shapes,
        in_specs=[ANY] * len(arrays),
        out_specs=[ANY] * len(arrays),
        scratch_shapes=[
            dma((units, max(Z - 1, 1))),
            dma((units, max(Z * (Y - 1), 1))),
            dma((units,)),
            dma((units,)),
            dma((units,)),
            dma((len(arrays),)),
            dma((len(arrays),)),
        ],
        compiler_params=pltpu.CompilerParams(collective_id=0, has_side_effects=True),
    )(*arrays)


def add_blocks(rows, terms, out, out_type):
    chunk = 16 if rows % 16 == 0 else rows

    def body(i, _):
        part = pl.ds(pl.multiple_of(i * chunk, chunk), chunk)
        total = terms[0][part, :].astype(f32)
        for term in terms[1:]:
            total = total + term[part, :].astype(f32)
        out[part, :] = total.astype(out_type)
        return _

    lax.fori_loop(0, rows // chunk, body, 0)


def scatter_kernel(n, count, *refs):
    sources, outs = refs[:count], refs[count : 2 * count]
    scratch = refs[2 * count :]
    mine, from_c, from_y, from_z = (scratch[k * count : (k + 1) * count] for k in range(4))
    l_sem, cs_sem, cr_sem, ys_sem, yr_sem, zs_sem, zr_sem = scratch[4 * count :]
    at = Place(n)
    Z, Y = at.Z, at.Y
    greet(at.partners()[:-1])

    c_copies, l_copies, y_copies, z_copies = [], [], [], []
    for i in range(count):
        copy = remote(
            sources[i].at[:, 1 - at.c],
            from_c[i],
            cs_sem.at[i],
            cr_sem.at[i],
            at.device(at.z, at.y, 1 - at.c),
        )
        copy.start()
        c_copies.append(copy)
        copy = pltpu.make_async_copy(sources[i].at[:, at.c], mine[i], l_sem.at[i])
        copy.start()
        l_copies.append(copy)

    def after_core(i):
        c_copies[i].wait_recv()
        l_copies[i].wait()
        rows = mine[i].shape[1]
        for k in list(range(1, Y)) + [0]:
            y = at.along_y(k)

            def per_z(z, _):
                zy = z * Y + y
                add_blocks(rows, [mine[i].at[zy], from_c[i].at[zy]], mine[i].at[zy], mine[i].dtype)
                return _

            lax.fori_loop(0, Z, per_z, 0)
            if k:
                for z in range(Z):
                    copy = remote(
                        mine[i].at[z * Y + y],
                        from_y[i].at[k - 1, z],
                        ys_sem.at[i, k - 1, z],
                        yr_sem.at[i, k - 1, z],
                        at.device(at.z, y, at.c),
                    )
                    copy.start()
                    y_copies.append(copy)

    def after_y(i):
        rows = mine[i].shape[1]
        for k in list(range(1, Z)) + [0]:
            z = at.along_z(k)
            block = mine[i].at[z * Y + at.y]
            for j in range(1, Y):
                arrival(from_y[i].at[j - 1, z], yr_sem.at[i, j - 1, z]).wait()
            terms = [block] + [from_y[i].at[j - 1, z] for j in range(1, Y)]
            add_blocks(rows, terms, block, mine[i].dtype)
            if k:
                copy = remote(
                    block,
                    from_z[i].at[k - 1],
                    zs_sem.at[i, k - 1],
                    zr_sem.at[i, k - 1],
                    at.device(z, at.y, at.c),
                )
                copy.start()
                z_copies.append(copy)

    def after_z(i):
        rows = mine[i].shape[1]
        for k in range(1, Z):
            arrival(from_z[i].at[k - 1], zr_sem.at[i, k - 1]).wait()
        terms = [mine[i].at[at.zy]] + [from_z[i].at[k - 1] for k in range(1, Z)]
        add_blocks(rows, terms, outs[i], outs[i].dtype)

    for turn in range(count + 2):
        if turn < count:
            after_core(turn)
        if 0 <= turn - 1 < count:
            after_y(turn - 1)
        if turn - 2 >= 0:
            after_z(turn - 2)
    for copy in c_copies + y_copies + z_copies:
        copy.wait_send()


def scatter(n, arrays):
    Z, Y = factors(n)
    count = len(arrays)
    blocks = [a.shape[-2:] for a in arrays]
    arrays = [a.reshape((Z * Y, 2) + b) for a, b in zip(arrays, blocks)]
    dma = pltpu.SemaphoreType.DMA
    scratch = [pltpu.VMEM((Z * Y,) + b, a.dtype) for a, b in zip(arrays, blocks)]
    scratch += [pltpu.VMEM((Z * Y,) + b, a.dtype) for a, b in zip(arrays, blocks)]
    scratch += [pltpu.VMEM((max(Y - 1, 1), Z) + b, a.dtype) for a, b in zip(arrays, blocks)]
    scratch += [pltpu.VMEM((max(Z - 1, 1),) + b, a.dtype) for a, b in zip(arrays, blocks)]
    return pl.pallas_call(
        functools.partial(scatter_kernel, n, count),
        out_shape=[jax.ShapeDtypeStruct(b, f32) for b in blocks],
        in_specs=[ANY] * count,
        out_specs=[VMEM] * count,
        scratch_shapes=scratch
        + [
            dma((count,)),
            dma((count,)),
            dma((count,)),
            dma((count, max(Y - 1, 1), Z)),
            dma((count, max(Y - 1, 1), Z)),
            dma((count, max(Z - 1, 1))),
            dma((count, max(Z - 1, 1))),
        ],
        compiler_params=pltpu.CompilerParams(
            collective_id=1, has_side_effects=True, vmem_limit_bytes=VMEM_LIMIT
        ),
    )(*arrays)


def forward_kernel(emb, wi, wr, ctx, keep, z_o, r_o, n_o, m_o, p_o, h_o, drive):
    R, H = ctx.shape[0], wr.shape[0]
    drive[...] = nt(emb[...], wi[...])

    def step(t, h):
        rows = pl.ds(pl.multiple_of(t * R, R), R)
        p = h * keep[rows, :]
        p_o[rows, :] = p
        rec = nn(p.astype(bf16), wr[...])
        d = drive[rows, :]
        z = jax.nn.sigmoid(d[:, :H] + rec[:, :H] + ctx[:, :H])
        r = jax.nn.sigmoid(d[:, H : 2 * H] + rec[:, H : 2 * H] + ctx[:, H : 2 * H])
        m = rec[:, 2 * H :] + ctx[:, 2 * H :]
        n = jnp.tanh(d[:, 2 * H :] + r * m)
        h = z * p + (1.0 - z) * n
        z_o[rows, :] = z
        r_o[rows, :] = r
        n_o[rows, :] = n
        m_o[rows, :] = m
        h_o[rows, :] = h.astype(bf16)
        return h

    lax.fori_loop(0, emb.shape[0] // R, step, jnp.zeros((R, H), f32))


def gru_forward(emb, wi, wr, ctx, keep):
    tokens, H = emb.shape[0], wr.shape[0]
    shape = jax.ShapeDtypeStruct
    return pl.pallas_call(
        forward_kernel,
        out_shape=[shape((tokens, H), f32)] * 5 + [shape((tokens, H), bf16)],
        in_specs=[VMEM] * 5,
        out_specs=[VMEM] * 6,
        scratch_shapes=[pltpu.VMEM((tokens, 3 * H), f32)],
        compiler_params=pltpu.CompilerParams(vmem_limit_bytes=VMEM_LIMIT),
    )(emb, wi, wr, ctx, keep)


def backward_kernel(sg, carry0, keep, z, r, n, m, p, wr, low_o, cand_o, sum_o):
    R, H = carry0.shape
    steps = sg.shape[0] // R

    def step(i, carry):
        rows = pl.ds(pl.multiple_of((steps - 1 - i) * R, R), R)
        g = sg[rows, :] + carry
        zz = z[rows, :]
        cand = n[rows, :]
        rr = r[rows, :]
        pc = g * (1.0 - zz) * (1.0 - cand * cand)
        pz = g * (p[rows, :] - cand) * zz * (1.0 - zz)
        pr = pc * m[rows, :] * rr * (1.0 - rr)
        rec = jnp.concatenate([pz, pr, pc * rr], axis=1)
        low = rec.astype(bf16)
        low_o[rows, :] = low
        cand_o[rows, :] = pc.astype(bf16)
        sum_o[...] += rec
        return (g * zz + nt(low, wr[...])) * keep[rows, :]

    sum_o[...] = jnp.zeros_like(sum_o)
    lax.fori_loop(0, steps, step, carry0[...])


def gru_backward(sg, carry0, keep, record, wr):
    z, r, n, m, p = record
    tokens, H = sg.shape
    shape = jax.ShapeDtypeStruct
    return pl.pallas_call(
        backward_kernel,
        out_shape=[
            shape((tokens, 3 * H), bf16),
            shape((tokens, H), bf16),
            shape((carry0.shape[0], 3 * H), f32),
        ],
        in_specs=[VMEM] * 9,
        out_specs=[VMEM] * 3,
        compiler_params=pltpu.CompilerParams(vmem_limit_bytes=VMEM_LIMIT),
    )(sg, carry0, keep, z, r, n, m, p, wr)


def request_slots(ids, n, per, slots):
    count = ids.shape[0]
    index = jnp.arange(count, dtype=jnp.int32)
    same = ids[:, None] == ids[None, :]
    first = jnp.min(jnp.where(same, index[None, :], count), axis=1)
    leads = first == index
    owner = ids // per
    ahead = (owner[:, None] == owner[None, :]) & leads[None, :] & (index[None, :] < first[:, None])
    rank = jnp.sum(ahead.astype(jnp.int32), axis=1)
    return leads, owner, rank, ids - owner * per


def round_maps(plan, turn, n, slots):
    leads, owner, rank, local = plan
    place = rank - turn * slots
    inside = (place >= 0) & (place < slots)
    place = jnp.where(inside, owner * slots + place, -1)
    hit = place[:, None] == jnp.arange(n * slots, dtype=jnp.int32)[None, :]
    asked = jnp.max(jnp.where(hit & leads[:, None], local[:, None], -1), axis=0)
    return asked, hit.astype(bf16)


def swap(x, n):
    shape = x.shape
    return lax.all_to_all(x.reshape((n, -1) + shape[1:]), "dp", 0, 0, tiled=False).reshape(shape)


def owner_map(asked, n, per):
    asked_here = swap(asked, n)
    return (asked_here[:, None] == jnp.arange(per, dtype=jnp.int32)[None, :]).astype(bf16)


def per_device(
    token_ids,
    resets,
    targets,
    embedding,
    input_gates,
    recur_gates,
    square,
    context_gates,
    deep_embed,
    deep_context,
    softmax_weight,
):
    n = lax.axis_size("dp")
    s = lax.axis_index("section")
    d = lax.axis_index("dp")
    is_decoder = s == 1
    micro, rows, steps = token_ids.shape[1:]
    R = micro * rows
    tokens = R * steps
    H = square.shape[2]
    E = embedding.shape[2]
    M = softmax_weight.shape[1]
    per = embedding.shape[1]
    slots = max(512 // n, 8)
    scale = 1.0 / (R * n)

    def time_major(x):
        return jnp.transpose(x.reshape(R, steps), (1, 0)).reshape(-1)

    ids = time_major(token_ids[0])
    keep = time_major(1 - resets[0]).astype(f32)[:, None]
    labels = time_major(targets)

    plan = request_slots(ids, n, per, slots)
    rounds = lax.pmax(jnp.max(plan[2]) // slots + 1, ("section", "dp"))
    table = embedding[0]

    def fetch(turn):
        asked, hit = round_maps(plan, turn, n, slots)
        owners = owner_map(asked, n, per)
        came = swap(nn(owners, table).astype(bf16), n)
        return owners, hit, nn(hit, came).astype(bf16)

    owners, hit, emb = fetch(0)

    def more(carry):
        turn, emb = carry
        return turn + 1, emb + fetch(turn)[2]

    _, emb = lax.while_loop(lambda c: c[0] < rounds, more, (jnp.int32(1), emb))

    wr, wi, sq, sm, cg, de, dc = gather(
        n,
        [
            recur_gates[0],
            input_gates[0],
            square[0],
            softmax_weight,
            context_gates,
            deep_embed,
            deep_context,
        ],
        (False, False, False, False, True, True, True),
    )
    wr, wi, sq, sm = wr.reshape(H, 3 * H), wi.reshape(3 * H, E), sq.reshape(H, H), sm.reshape(-1, M)
    cg, de, dc = cg.reshape(H, 3 * H), de.reshape(2 * M, E), dc.reshape(H, 2 * M)

    enc = gru_forward(emb, wi, wr, jnp.zeros((R, 3 * H), f32), keep)
    last_low = enc[5][-R:]
    ctx_tanh = jnp.tanh(nn(last_low, sq))
    context = lax.ppermute(ctx_tanh.astype(bf16), "section", [(0, 1)])

    dec = gru_forward(emb, wi, wr, nn(context, cg), keep)
    states_low = dec[5]
    deep_pre = nn(states_low, sq) + nt(emb, de)
    deep_pre = (deep_pre.reshape(steps, R, -1) + nn(context, dc)[None]).reshape(tokens, -1)
    smooth = jnp.logaddexp(deep_pre[:, :M], deep_pre[:, M:])
    smooth_low = smooth.astype(bf16)

    came = lax.ppermute(smooth_low, "section", [(1, 0)])
    head_in = jnp.where(is_decoder, smooth_low, came)
    words = sm.shape[0]
    logits = nt(head_in, sm)
    top = jnp.max(logits, axis=1)
    total = jnp.sum(jnp.exp(logits - top[:, None]), axis=1)
    hits = lax.broadcasted_iota(jnp.int32, logits.shape, 1) == (labels - s * words)[:, None]
    picked = jnp.sum(jnp.where(hits, logits, 0.0), axis=1)
    stats = jnp.stack([top, total, picked])
    other = lax.ppermute(stats, "section", [(0, 1), (1, 0)])
    all_top = jnp.maximum(top, other[0])
    log_norm = all_top + jnp.log(
        total * jnp.exp(top - all_top) + other[1] * jnp.exp(other[0] - all_top)
    )
    loss = jnp.where(is_decoder, jnp.sum(log_norm - picked - other[2]) * scale, 0.0)
    logit_low = ((jnp.exp(logits - log_norm[:, None]) - hits.astype(f32)) * scale).astype(bf16)
    smooth_part = nn(logit_low, sm)
    smooth_grad = smooth_part + lax.ppermute(smooth_part, "section", [(0, 1)])
    softmax_term = tn(logit_low, head_in).astype(bf16)

    deep_grad = jnp.concatenate(
        [
            smooth_grad * jnp.exp(deep_pre[:, :M] - smooth),
            smooth_grad * jnp.exp(deep_pre[:, M:] - smooth),
        ],
        axis=1,
    )
    deep_low = deep_grad.astype(bf16)
    outer_low = jnp.sum(deep_grad.reshape(steps, R, -1), axis=0).astype(bf16)
    state_grad = nt(deep_low, sq)
    dec_low, dec_cand, drive_sum = gru_backward(
        state_grad, jnp.zeros((R, H), f32), keep, dec[:5], wr
    )
    drive_sum_low = drive_sum.astype(bf16)
    context_grad = (nt(outer_low, dc) + nt(drive_sum_low, cg)).astype(bf16)
    packed = lax.all_gather(jnp.concatenate([context, outer_low, drive_sum_low], axis=1), "dp", tiled=True)
    packed_came = lax.ppermute(packed, "section", [(1, 0)])
    packed = jnp.where(is_decoder, packed, packed_came)

    context_back = lax.ppermute(context_grad, "section", [(1, 0)])
    pre_low = (context_back.astype(f32) * (1.0 - ctx_tanh * ctx_tanh)).astype(bf16)
    enc_low, enc_cand, _ = gru_backward(
        jnp.zeros((tokens, H), f32), nt(pre_low, sq), keep, enc[:5], wr
    )

    def pick(of_encoder, of_decoder):
        return jnp.where(is_decoder, of_decoder, of_encoder)

    recur_low = pick(enc_low, dec_low)
    cand_low = pick(enc_cand, dec_cand)
    before_low = pick(enc[4], dec[4]).astype(bf16)
    drive_low = jnp.concatenate([recur_low[:, : 2 * H], cand_low], axis=1)
    recur_term = tn(before_low, recur_low).astype(bf16)
    input_term = tn(drive_low, emb).astype(bf16)
    deep_mask = jnp.where(is_decoder, deep_low, jnp.zeros_like(deep_low))
    input_grad = nn(drive_low, wi) + nn(deep_mask, de)
    rows_pad = jnp.zeros((tokens - R, H), bf16)
    square_term = tn(
        pick(jnp.concatenate([last_low, rows_pad]), states_low),
        pick(jnp.concatenate([pre_low, rows_pad]), deep_low),
    ).astype(bf16)
    deep_term = tn(deep_mask, emb).astype(bf16)

    input_grad_low = input_grad.astype(bf16)

    def give(owners, hit):
        return tn(owners, swap(tn(hit, input_grad_low).astype(bf16), n))

    def give_more(carry):
        turn, grad = carry
        asked, hit = round_maps(plan, turn, n, slots)
        return turn + 1, grad + give(owner_map(asked, n, per), hit)

    table_grad = give(owners, hit)
    _, table_grad = lax.while_loop(
        lambda c: c[0] < rounds, give_more, (jnp.int32(1), table_grad)
    )

    deep_blocks = jnp.stack(
        [x.reshape((n,) + deep_embed.shape) for x in jnp.split(deep_term, 2)], axis=1
    )
    deep_blocks = deep_blocks.reshape(n, 2 * deep_embed.shape[0], E)
    loss_blocks = jnp.broadcast_to(loss, (n, 8, 128))
    square_sum, recur_sum, input_sum, softmax_sum, deep_sum, loss_sum = scatter(
        n,
        [
            square_term.reshape((n,) + square.shape[1:]),
            recur_term.reshape((n,) + recur_gates.shape[1:]),
            input_term.reshape((n,) + input_gates.shape[1:]),
            softmax_term.reshape((n,) + softmax_weight.shape),
            deep_blocks,
            loss_blocks,
        ],
    )
    deep_halves = deep_sum.reshape((2,) + deep_embed.shape)
    both = lax.ppermute(
        jnp.concatenate([deep_halves[0].reshape(-1), loss_sum[:1].reshape(-1)]), "section", [(1, 0)]
    )
    deep_out = jnp.where(is_decoder, deep_halves[1], both[:-128].reshape(deep_embed.shape))
    loss_out = jnp.where(is_decoder, loss_sum[0, 0], both[-1])

    own = (s * n + d) * context_gates.shape[0]
    context_own = lax.dynamic_slice(packed, (0, own), (packed.shape[0], context_gates.shape[0]))
    gates_out = tn(context_own, packed[:, H + 2 * M :])
    context_out = tn(context_own, packed[:, H : H + 2 * M])

    return (
        loss_out,
        table_grad[None],
        input_sum[None],
        recur_sum[None],
        square_sum[None],
        gates_out,
        deep_out,
        context_out,
        softmax_sum,
    )


def solution(mesh):
    halves = P("section", "dp", None)
    whole = P(("section", "dp"), None)
    in_specs = (
        P("section", None, "dp", None),
        P("section", None, "dp", None),
        P(None, "dp", None),
        halves,
        halves,
        halves,
        halves,
        whole,
        whole,
        whole,
        whole,
    )
    out_specs = (P(), halves, halves, halves, halves, whole, whole, whole, whole)
    return jax.shard_map(
        per_device, mesh=mesh, in_specs=in_specs, out_specs=out_specs, check_vma=False
    )
```

time: 2270 us -> 826 us (0.36)
  waiting for transfers between devices: 1670 us -> 193 us
  Pallas kernels: 0 us -> 417 us
  matrix products: 241 us -> 58.3 us
  local copies, waits for them, and re-layouts: 164 us -> 32.5 us
  other arithmetic: 112 us -> 19.3 us
    reduce_scatter x8 -> x0, waiting for transfers between devices: 911 us -> none  [the longest x1 204 us: per_device(): lax.psum_scatter(half_terms[0], 'dp', scatter_dimension=0, tiled=True)]
    pallas_call x0 -> x6, Pallas kernels: none -> 417 us  [the longest x1 173 us: gather(): pl.pallas_call(functools.partial(gather_kernel, n, crossed), out_shape=sh...]
    ppermute x2 -> x7, waiting for transfers between devices: 474 us -> 146 us  [the longest x1 112 us: per_device(): context_back = lax.ppermute(context_grad, 'section', [(1, 0)])]
    all_gather x8 -> x1, waiting for transfers between devices: 281 us -> 47.1 us  [per_device(): lax.all_gather(jnp.concatenate([context, outer_low, drive_sum_low], axis=...]
    dot_general x62 -> x24, matrix products: 241 us -> 58.3 us  [the longest x9 25.7 us: tn(): lax.dot_general(a, b, (((0,), (0,)), ((), ())), preferred_element_type=f32)]
    another operation x45 -> x6, local copies, waits for them, and re-layouts: 63.3 us -> 2.21 us  [the longest x1 1.28 us: per_device(): jnp.stack([x.reshape((n,) + deep_embed.shape) for x in jnp.split(deep_ter...]
    dynamic_update_slice x72 -> x0, other arithmetic: 50.4 us -> none  [the longest x48 34.4 us: gru_forward(): lax.scan(advance, jnp.zeros((row_count, hidden), jnp.float32), (input_dri...]
    cond x20 -> x0, local copies, waits for them, and re-layouts: 48.8 us -> none  [the longest x3 27.3 us: per_device(): half_terms = lax.cond(is_encoder, encode_back, lambda: dec_terms)]
  transfers between devices with their start and end apart: 18 -> 10, of which waited for: 13 -> 6; matrix products, arithmetic and copies ran while one was open for 21% -> 7% of each run, Pallas kernels for 0% -> 41%
where the time goes in v1:
time: 826 us; the launch traced here: 817 us
  Pallas kernels  417 us (50%)
  waiting for transfers between devices  193 us (23%)
  matrix products  58.3 us (7%)
  blocking collectives  54.3 us (7%)
  local copies, waits for them, and re-layouts  32.5 us (4%)
  starting transfers between devices  20.8 us (3%)
  between operations  20.8 us (3%)
  other arithmetic  19.3 us (2%)
    pallas_call x1, Pallas kernels, gather(): pl.pallas_call(functools.partial(gather_kernel, n, crossed), out_shape=sh...  173 us
    pallas_call x1, Pallas kernels, scatter(): pl.pallas_call(functools.partial(scatter_kernel, n, count), out_shape=[ja...  136 us
    ppermute x1, waiting for transfers between devices, per_device(): context_back = lax.ppermute(context_grad, 'section', [(1, 0)])  112 us
    pallas_call x2, Pallas kernels, gru_backward(): pl.pallas_call(backward_kernel, out_shape=[shape((tokens, 3 * H), bf16),...  59.3 us
    pallas_call x2, Pallas kernels, gru_forward(): pl.pallas_call(forward_kernel, out_shape=[shape((tokens, H), f32)] * 5 +...  48.3 us
    all_gather x1, waiting for transfers between devices, per_device(): lax.all_gather(jnp.concatenate([context, outer_low, drive_sum_low], axis=...  47.1 us
    pmax x1, blocking collectives, per_device(): rounds = lax.pmax(jnp.max(plan[2]) // slots + 1, ('section', 'dp'))  40.7 us
    dot_general x9, matrix products, tn(): lax.dot_general(a, b, (((0,), (0,)), ((), ())), preferred_element_type=f32)  25.7 us
  transfers between devices with their start and end apart: 10, of which 6 were waited for; matrix products, arithmetic and copies ran while one was open for 7% of the time, Pallas kernels for 41%

profile of v1, /device:TPU:0, one launch (start us, length us, event | category | flops | bytes accessed | tf_op | source)
XLA Modules:
  0.0 817.1 jit_solution(12783755626859114629)
XLA Ops:
  9.6 13.6 %all_to_all.53 = s32[16,1,32]{2,1,0:T(1,128)S(1)} all-to-all(s32[16,1,32]{2,1,0:T(1,128)S(1)} %all_to_all.30), channel_id=1, replica_groups=mesh['section'=2,'dp'=16] {'dp'}, dimensions={0} | all-to-all | bytes 4096 | tf_op jit(solution)/shard_map/all_to_all | solution.py:421
  24.5 1.8 convolution_convert_fusion.9
  27.3 3.7 all-to-all-start.5
  33.7 40.7 %pmax.7 = s32[]{:T(128)} all-reduce(s32[]{:T(128)S(6)} %add.106), channel_id=1, replica_groups=mesh['section'=2,'dp'=16] {'section','dp'}, use_global_device_ids=true, to_apply=%region_4.5 | all-reduce | flops 1 | bytes 8 | tf_op jit(solution)/shard_map/pmax | solution.py:464
  75.4 173.2 %shard_map.178 = (bf16[8,2,64,3072]{3,2,1,0:T(8,128)(2,1)}, bf16[8,2,192,620]{3,2,1,0:T(8,128)(2,1)}, bf16[8,2,64,1024]{3,2,1,0:T(8,128)(2,1)}, bf16[8,2,240,512...) custom-call(bf16[64,3072]{1,0:T(8,128)(2,1)} %bitcast.136, ...), custom_call_target="tpu_custom_call" | custom-call | tf_op jit(solution)/shard_map/pallas_call | solution.py:168
  251.8 24.2 %shard_map.179 = (f32[384,1024]{1,0:T(8,128)}, f32[384,1024]{1,0:T(8,128)}, f32[384,1024]{1,0:T(8,128)}, f32[384,1024]{1,0:T(8,128)}, f32[384,1024]{1,0:T(8,128)}, /*index=5*/bf16[384,1024]{1,0:T(8,128)(2,1)}) custom-call(bf16[384,620]{1,0:T(8,128)(2,1)} %copy.46.emb, bf16[3072,620]{1,0:T(8,128)(2,1)} %bitcast.116, bf16[1024,3072]{1,0:T(8,128)(2,1)} %bitcast.100, ...), custom_call_target="tpu_custom_call" | custom-call | tf_op jit(solution)/shard_map/pallas_call | solution.py:346
  276.0 1.4 fusion.48
  277.4 5.6 collective-permute-start
  283.0 2.0 fusion.51
  285.0 4.7 fusion.50.ctx
  289.7 24.1 %shard_map.180 = (f32[384,1024]{1,0:T(8,128)}, f32[384,1024]{1,0:T(8,128)}, f32[384,1024]{1,0:T(8,128)}, f32[384,1024]{1,0:T(8,128)}, f32[384,1024]{1,0:T(8,128)}, /*index=5*/bf16[384,1024]{1,0:T(8,128)(2,1)}) custom-call(bf16[384,620]{1,0:T(8,128)(2,1)} %copy.46.emb, bf16[3072,620]{1,0:T(8,128)(2,1)} %bitcast.117, bf16[1024,3072]{1,0:T(8,128)(2,1)} %bitcast.101, ...), custom_call_target="tpu_custom_call" | custom-call | tf_op jit(solution)/shard_map/pallas_call | solution.py:346
  313.8 2.2 fusion.52
  316.0 2.1 bitcast_add_fusion
  321.3 11.6 %collective-permute-done.1 = bf16[384,512]{1,0:T(8,128)(2,1)} collective-permute-done((bf16[384,512]{1,0:T(8,128)(2,1)S(1)}, bf16[384,512]{1,0:T(8,128)(2,1)}, u32[]{:S(2)}, u32[]{:S(2)}) %collective-permute-start.1) | collective-permute-done | bytes 393248 | tf_op jit(solution)/shard_map/ppermute | solution.py:509
  332.9 4.1 fusion.49
  336.9 1.6 exponential_reduce_fusion
  338.7 3.6 collective-permute-done.2
  343.0 2.0 multiply_convert_fusion
  345.1 1.7 fusion.53
  346.8 2.1 collective-permute-start.3
  348.9 15.1 %collective-permute-done.3 = f32[384,512]{1,0:T(8,128)S(1)} collective-permute-done((f32[384,512]{1,0:T(8,128)S(1)}, f32[384,512]{1,0:T(8,128)S(1)}, u32[]{:S(2)}, u32[]{:S(2)}) %collective-permute-start.3) | collective-permute-done | bytes 786464 | tf_op jit(solution)/shard_map/ppermute | solution.py:526
  364.8 1.4 pad_maximum_fusion.1
  366.2 2.2 fusion.55.sg
  369.1 29.7 %shard_map.181 = (bf16[384,3072]{1,0:T(8,128)(2,1)}, bf16[384,1024]{1,0:T(8,128)(2,1)}, f32[32,3072]{1,0:T(8,128)}) custom-call(f32[384,1024]{1,0:T(8,128)} %fusion.55.sg, f32[32,1024]{1,0:T(8,128)} %broadcast_in_dim.118.carry0, f32[384,1]{1,0:T(8,128)} %convert_element_type.122.keep, f32[384,1024]{1,0:T(8,128)} %get-tuple-element.135.z, ...), custom_call_target="tpu_custom_call" | custom-call | tf_op jit(solution)/shard_map/pallas_call | solution.py:384
  399.8 1.7 reduce_sum.48
  403.8 6.2 convolution_convert_fusion.3
  410.6 1.9 convolution_convert_fusion.7
  412.6 2.0 fusion.11
  414.5 47.1 %all-gather.2.cloned.1.call-done = bf16[512,5120]{1,0:T(8,128)(2,1)} async-done(((bf16[32,5120]{1,0:T(8,128)(2,1)}), bf16[512,5120]{1,0:T(8,128)(2,1)}) %all-gather.2.cloned.1.call-update) | async-done | bytes 5242896 | tf_op jit(solution)/shard_map/all_gather | solution.py:544
  462.9 1.4 fusion.46
  464.8 1.5 collective-permute-start.4
  467.8 112.5 %collective-permute-done.4 = bf16[32,1024]{1,0:T(8,128)(2,1)S(1)} collective-permute-done((bf16[32,1024]{1,0:T(8,128)(2,1)S(1)}, bf16[32,1024]{1,0:T(8,128)(2,1)S(1)}, u32[]{:S(2)}, u32[]{:S(2)}) %collective-permute-start.4) | collective-permute-done | bytes 65568 | tf_op jit(solution)/shard_map/ppermute | solution.py:548
  580.3 1.4 fusion.56.carry0
  581.7 1.4 broadcast_in_dim.119.sg
  583.1 29.7 %shard_map.182 = (bf16[384,3072]{1,0:T(8,128)(2,1)}, bf16[384,1024]{1,0:T(8,128)(2,1)}, f32[32,3072]{1,0:T(8,128)}) custom-call(f32[384,1024]{1,0:T(8,128)} %broadcast_in_dim.119.sg, f32[32,1024]{1,0:T(8,128)} %fusion.56.carry0, f32[384,1]{1,0:T(8,128)} %convert_element_type.122.keep, f32[384,1024]{1,0:T(8,128)} %get-tuple-element.143.z, ...), custom_call_target="tpu_custom_call" | custom-call | tf_op jit(solution)/shard_map/pallas_call | solution.py:384
  612.8 1.9 broadcast_select_fusion.1
  617.6 4.0 convolution_convert_fusion.5
  621.6 6.2 copy.50
  627.9 4.9 fusion.9
  636.2 7.1 convolution_convert_fusion.4
  643.3 3.8 all-to-all-start.6
  647.1 2.7 convolution_convert_fusion.6
  650.4 136.1 %shard_map.183 = (f32[64,1024]{1,0:T(8,128)}, f32[64,3072]{1,0:T(8,128)}, f32[192,620]{1,0:T(8,128)}, f32[240,512]{1,0:T(8,128)}, f32[64,620]{1,0:T(8,128)}, /*index=5*/f32[8,128]{1,0:T(8,128)}) custom-call(bf16[8,2,64,1024]{3,2,1,0:T(8,128)(2,1)} %bitcast.130, bf16[8,2,64,3072]{3,2,1,0:T(8,128)(2,1)} %bitcast.121, bf16[8,2,192,620]{3,2,1,0:T(8,128)(2,1)} %bitcast.115, ...), custom_call_target="tpu_custom_call" | custom-call | tf_op jit(solution)/shard_map/pallas_call | solution.py:297
  788.2 1.3 collective-permute-start.5
  791.7 2.8 collective-permute-done.5
  796.6 1.5 slice_select_fusion
  798.8 3.0 broadcast_select_fusion
  801.9 1.5 fusion.7
  (135 shorter events, 38.4 us)
Async XLA Ops:
  7.2 67.3 %copy-start.26 = (s32[1,2,16,12]{2,1,3,0:T(2,128)S(1)}, s32[1,2,16,12]{2,1,3,0:T(2,128)}, u32[]{:S(2)}) copy-start(s32[1,2,16,12]{2,1,3,0:T(2,128)} %param.16) | copy-start | bytes 4612
  27.3 222.0 %copy-start.28 = (bf16[1,480,620]{2,1,0:T(8,128)(2,1)S(1)}, bf16[1,480,620]{2,1,0:T(8,128)(2,1)}, u32[]{:S(2)}) copy-start(bf16[1,480,620]{2,1,0:T(8,128)(2,1)} %param.18) | copy-start | bytes 1785604
  27.3 221.3 %all-to-all-start.5 = ((bf16[16,32,620]{2,1,0:T(8,128)(2,1)}), bf16[16,32,620]{2,1,0:T(8,128)(2,1)S(1)}, u32[]{:S(2)}, u32[]{:S(2)}) async-start(bf16[16,32,620]{2,1,0:T(8,128)(2,1)} %bitcast.6), calls=%async_computation.5 | async-start | bytes 1310720 | tf_op jit(solution)/shard_map/all_to_all | solution.py:421
  31.1 430.5 %all-gather.2.cloned.1.call-start = ((), (), s32[]{:S(2)}) async-start(), calls=%async_computation.7 | async-start | bytes 5570560 | tf_op jit(solution)/shard_map/all_gather | solution.py:544
  251.8 24.2 %copy-start.1 = (bf16[8,2,64,1024]{3,2,1,0:T(8,128)(2,1)S(1)}, bf16[8,2,64,1024]{3,2,1,0:T(8,128)(2,1)}, u32[]{:S(2)}) copy-start(bf16[8,2,64,1024]{3,2,1,0:T(8,128)(2,1)} %get-tuple-element.129) | copy-start | bytes 6291460
  276.0 7.0 copy-start.10
  277.4 7.6 collective-permute-start
  313.8 2.2 copy-start.6
  316.0 5.1 copy-start.27
  318.1 1.2 copy-start.3
  319.8 13.1 %collective-permute-start.1 = (bf16[384,512]{1,0:T(8,128)(2,1)S(1)}, bf16[384,512]{1,0:T(8,128)(2,1)}, u32[]{:S(2)}, u32[]{:S(2)}) collective-permute-start(bf16[384,512]{1,0:T(8,128)(2,1)S(1)} %fusion.45), channel_id=1, source_target_pairs={{16,0},{17,1},{18,2},{19,3},{20,4},{21,5},{22,6},{23,7},{24,8},{25... | collective-permute-start | bytes 1179656 | tf_op jit(solution)/shard_map/ppermute | solution.py:509
  338.6 3.7 collective-permute-start.2
  343.0 2.1 copy-start.7
  345.1 1.7 copy-start.8
  345.1 18.9 %copy-start.4 = (f32[384,1024]{1,0:T(8,128)S(1)}, f32[384,1024]{1,0:T(8,128)}, u32[]{:S(2)}) copy-start(f32[384,1024]{1,0:T(8,128)} %copy-done.3) | copy-start | bytes 4718596
  346.8 17.2 %collective-permute-start.3 = (f32[384,512]{1,0:T(8,128)S(1)}, f32[384,512]{1,0:T(8,128)S(1)}, u32[]{:S(2)}, u32[]{:S(2)}) collective-permute-start(f32[384,512]{1,0:T(8,128)S(1)} %fusion.53), channel_id=1, source_target_pairs={{0,16},{1,17},{2,18},{3,19},{4,20},{5,21},{6,22},{7,23},{8,24},{9,... | collective-permute-start | bytes 2359304 | tf_op jit(solution)/shard_map/ppermute | solution.py:526
  364.8 3.6 copy-start.18
  399.8 12.8 %slice-start = ((s8[6291456]{0:T(1024)(128)(4,1)}), s8[2097152]{0:T(1024)(128)(4,1)S(1)}, s32[]{:S(2)}) async-start(s8[6291456]{0:T(1024)(128)(4,1)} %bitcast.107), calls=%async_computation.8 | async-start | bytes 4194304
  403.7 6.2 copy-start.5
  403.7 6.9 copy-start.19
  403.7 8.8 %slice-start.1 = ((s8[6291456]{0:T(1024)(128)(4,1)}), s8[4194304]{0:T(1024)(128)(4,1)S(1)}, s32[]{:S(2)}) async-start(s8[6291456]{0:T(1024)(128)(4,1)} %bitcast.107), calls=%async_computation.9 | async-start | bytes 8388608
  461.6 337.2 %collective-permute-start.6 = (bf16[512,5120]{1,0:T(8,128)(2,1)}, bf16[512,5120]{1,0:T(8,128)(2,1)}, u32[]{:S(2)}, u32[]{:S(2)}) collective-permute-start(bf16[512,5120]{1,0:T(8,128)(2,1)} %all-gather.2.cloned.1.call-done), channel_id=1, source_target_pairs={{16,0},{17,1},{18,2},{19,3},{20,4},{21,5},{22,6},{23,7},{24,8},{25... | collective-permute-start | bytes 15728648 | tf_op jit(solution)/shard_map/ppermute | solution.py:545
  464.8 115.5 %collective-permute-start.4 = (bf16[32,1024]{1,0:T(8,128)(2,1)S(1)}, bf16[32,1024]{1,0:T(8,128)(2,1)S(1)}, u32[]{:S(2)}, u32[]{:S(2)}) collective-permute-start(bf16[32,1024]{1,0:T(8,128)(2,1)S(1)} %fusion.11), channel_id=1, source_target_pairs={{16,0},{17,1},{18,2},{19,3},{20,4},{21,5},{22,6},{23,7},{24,8},{25... | collective-permute-start | bytes 196616 | tf_op jit(solution)/shard_map/ppermute | solution.py:548
  466.3 114.0 %copy-start.2 = (bf16[8,2,64,1024]{3,2,1,0:T(8,128)(2,1)S(1)}, bf16[8,2,64,1024]{3,2,1,0:T(8,128)(2,1)}, u32[]{:S(2)}) copy-start(bf16[8,2,64,1024]{3,2,1,0:T(8,128)(2,1)} %get-tuple-element.129) | copy-start | bytes 6291460
  614.7 1.3 copy-start.13
  614.7 1.9 copy-start.14
  614.8 1.9 copy-start.9
  616.7 0.9 copy-start.15
  621.6 6.2 copy-start.16
  627.9 4.9 copy-start.11
  627.9 4.9 copy-start.20
  633.7 0.8 copy-start.23
  636.2 10.9 %copy-start.12 = (bf16[384,1024]{1,0:T(8,128)(2,1)S(1)}, bf16[384,1024]{1,0:T(8,128)(2,1)}, u32[]{:S(2)}) copy-start(bf16[384,1024]{1,0:T(8,128)(2,1)} %get-tuple-element.131) | copy-start | bytes 2359300
  643.3 154.9 %all-to-all-start.6 = ((bf16[16,32,620]{2,1,0:T(8,128)(2,1)}), bf16[16,32,620]{2,1,0:T(8,128)(2,1)S(1)}, u32[]{:S(2)}, u32[]{:S(2)}) async-start(bf16[16,32,620]{2,1,0:T(8,128)(2,1)} %bitcast.32), calls=%async_computation.6 | async-start | bytes 1310720 | tf_op jit(solution)/shard_map/all_to_all | solution.py:421
  650.4 139.1 %copy-start.24 = (bf16[384,620]{0,1:T(8,128)(2,1)S(1)}, bf16[384,620]{0,1:T(8,128)(2,1)}, u32[]{:S(2)}) copy-start(bf16[384,620]{0,1:T(8,128)(2,1)} %copy-done.23) | copy-start | bytes 1428484
  788.2 6.3 collective-permute-start.5
  804.4 1.0 copy-start.22
  804.4 1.8 copy-start.17
  805.2 3.4 copy-start
  805.2 1.9 copy-start.25
  805.2 2.6 copy-start.21
Sparse Core Ops, SparseCore 0:
  402.3 59.2 all-gather.1

commit v2 on v1

--- a/solution.py
+++ b/solution.py
@@ -284,7 +284,7 @@
         copy.wait_send()
 
 
-def scatter(n, arrays):
+def scatter(n, arrays, collective_id):
     Z, Y = factors(n)
     count = len(arrays)
     blocks = [a.shape[-2:] for a in arrays]
@@ -310,12 +310,12 @@
             dma((count, max(Z - 1, 1))),
         ],
         compiler_params=pltpu.CompilerParams(
-            collective_id=1, has_side_effects=True, vmem_limit_bytes=VMEM_LIMIT
+            collective_id=collective_id, has_side_effects=True, vmem_limit_bytes=VMEM_LIMIT
         ),
     )(*arrays)
 
 
-def forward_kernel(emb, wi, wr, ctx, keep, z_o, r_o, n_o, m_o, p_o, h_o, drive):
+def scan_kernel(emb, wi, wr, ctx, keep, z_o, r_o, n_o, m_o, p_o, h_o, drive):
     R, H = ctx.shape[0], wr.shape[0]
     drive[...] = nt(emb[...], wi[...])
 
@@ -344,7 +344,7 @@
     tokens, H = emb.shape[0], wr.shape[0]
     shape = jax.ShapeDtypeStruct
     return pl.pallas_call(
-        forward_kernel,
+        scan_kernel,
         out_shape=[shape((tokens, H), f32)] * 5 + [shape((tokens, H), bf16)],
         in_specs=[VMEM] * 5,
         out_specs=[VMEM] * 6,
@@ -426,7 +426,516 @@
     return (asked_here[:, None] == jnp.arange(per, dtype=jnp.int32)[None, :]).astype(bf16)
 
 
-def per_device(
+def multiple(x, of):
+    return pl.multiple_of(x, of)
+
+
+class Unit:
+    def __init__(self, index, src, dst, rows, base):
+        self.index, self.src, self.dst, self.rows, self.base = index, src, dst, rows, base
+
+    def block(self, zy, c):
+        return self.dst.at[pl.ds(multiple(self.base + (zy * 2 + c) * self.rows, 16), self.rows)]
+
+    def some(self, count):
+        return self.dst.at[pl.ds(0, count * self.rows)]
+
+
+class Gather:
+    def __init__(self, at, z_sem, y_sem, c_sem, s_sem):
+        self.at, self.z_sem, self.y_sem, self.c_sem, self.s_sem = at, z_sem, y_sem, c_sem, s_sem
+
+    def to_y(self, u, src, dst, slot):
+        at = self.at
+        for k in range(1, at.Y):
+            remote(
+                src,
+                dst,
+                self.s_sem.at[u.index],
+                self.y_sem.at[u.index, slot * (at.Y - 1) + k - 1],
+                at.device(at.z, at.along_y(k), at.c),
+            ).start()
+
+    def to_core(self, u, src, dst):
+        at = self.at
+        remote(
+            src, dst, self.s_sem.at[u.index], self.c_sem.at[u.index], at.device(at.z, at.y, 1 - at.c)
+        ).start()
+
+    def begin(self, u):
+        at = self.at
+        dst = u.block(at.zy, at.c)
+        self.to_y(u, u.src, dst, 0)
+        for k in range(1, at.Z):
+            remote(
+                u.src,
+                dst,
+                self.s_sem.at[u.index],
+                self.z_sem.at[u.index, k - 1],
+                at.device(at.along_z(k), at.y, at.c),
+            ).start()
+        self.to_core(u, u.src, dst)
+
+    def pass_z(self, u):
+        at = self.at
+        for k in range(1, at.Z):
+            block = u.block(at.along_z(-k) * at.Y + at.y, at.c)
+            arrival(block, self.z_sem.at[u.index, k - 1]).wait()
+            self.to_y(u, block, block, k)
+            self.to_core(u, block, block)
+
+    def pass_y(self, u):
+        at = self.at
+        for slot in range(at.Z):
+            for k in range(1, at.Y):
+                block = u.block(at.along_z(-slot) * at.Y + at.along_y(-k), at.c)
+                arrival(block, self.y_sem.at[u.index, slot * (at.Y - 1) + k - 1]).wait()
+                self.to_core(u, block, block)
+
+    def end(self, u):
+        blocks = self.at.Z * self.at.Y
+        part = u.some(blocks)
+        arrival(part, self.c_sem.at[u.index]).wait()
+        part = u.some(2 * blocks - 1)
+        arrival(part, self.s_sem.at[u.index]).wait()
+
+
+def forward_kernel(n, sizes, *refs):
+    R, H, E, M, slots, per, words = sizes
+    (
+        asked,
+        hit,
+        table,
+        keep,
+        labels,
+        wr_s,
+        wi_s,
+        sq_s,
+        sm_s,
+        cg_s,
+        de_s,
+        dc_s,
+    ) = refs[:12]
+    (
+        wr_o,
+        wi_o,
+        sq_o,
+        cg_o,
+        de_o,
+        dc_o,
+        term_o,
+        rec_o,
+        h_o,
+        emb_o,
+        pre_o,
+        grad_o,
+        tanh_o,
+        ctx_o,
+        loss_o,
+        most_o,
+        owners_o,
+    ) = refs[12:29]
+    (
+        asked_in,
+        rows_out,
+        came,
+        wr,
+        wi,
+        sq,
+        sm,
+        cg,
+        de,
+        dc,
+        drive,
+        rec,
+        smooth_in,
+        grad_out,
+        m_part,
+        s_part,
+        p_part,
+        fullest,
+        z_sem,
+        y_sem,
+        c_sem,
+        s_sem,
+        l_sem,
+        o_sem,
+        x_recv,
+        x_send,
+        as_sem,
+        ar_sem,
+        rs_sem,
+        rr_sem,
+    ) = refs[29:]
+    at = Place(n)
+    tokens = hit.shape[0]
+    steps = tokens // R
+    is_decoder = at.s == 1
+    beside = (1 - at.s, at.d)
+    others = [lax.rem(at.d + k, n) for k in range(1, n)]
+    greet([(at.s, d) for d in others] + [beside])
+
+    def block_rows(ref, base, rows):
+        return ref.at[pl.ds(multiple((base + at.d) * rows, 16), rows)]
+
+    def to_beside(src, dst, k):
+        return remote(src, dst, x_send.at[k], x_recv.at[k], beside)
+
+    gather = Gather(at, z_sem, y_sem, c_sem, s_sem)
+    u_wr = Unit(0, wr_s, wr, wr_s.shape[0], 0)
+    u_wi = Unit(1, wi_s, wi, wi_s.shape[0], 0)
+    u_sq = Unit(2, sq_s, sq, sq_s.shape[0], 0)
+    own_sm = Unit(3, sm_s, sm, words, 0)
+    far_sm = Unit(4, block_rows(sm, n, words), sm, words, n * words)
+    crossed = []
+    for k, (src, dst) in enumerate([(cg_s, cg), (de_s, de), (dc_s, dc)]):
+        rows = src.shape[0]
+        crossed.append(
+            (
+                Unit(3 + 2 * k, src, dst, rows, n * rows),
+                Unit(4 + 2 * k, block_rows(dst, 0, rows), dst, rows, 0),
+            )
+        )
+
+    asked_sends = []
+    for k, d in enumerate(others):
+        copy = remote(asked.at[d], asked_in.at[at.d], as_sem, ar_sem, (at.s, d))
+        copy.start()
+    gather.begin(u_wi)
+    gather.begin(u_wr)
+
+    @pl.when(is_decoder)
+    def _():
+        to_beside(sm_s, block_rows(sm, n, words), 0).start()
+
+    @pl.when(jnp.logical_not(is_decoder))
+    def _():
+        for k, (src, dst) in enumerate([(cg_s, cg), (de_s, de), (dc_s, dc)]):
+            to_beside(src, block_rows(dst, 0, src.shape[0]), 1 + k).start()
+
+    locals_ = [
+        pltpu.make_async_copy(src, block_rows(dst, 0, src.shape[0]), l_sem.at[k])
+        for k, (src, dst) in enumerate([(wr_s, wr), (wi_s, wi), (sq_s, sq)])
+    ]
+    locals_.append(pltpu.make_async_copy(sm_s, block_rows(sm, 0, words), l_sem.at[3]))
+    for k, (src, dst) in enumerate([(cg_s, cg), (de_s, de), (dc_s, dc)]):
+        locals_.append(pltpu.make_async_copy(src, block_rows(dst, n, src.shape[0]), l_sem.at[4 + k]))
+    for copy in locals_:
+        copy.start()
+
+    some_asked = asked_in.at[pl.ds(0, n - 1)]
+    arrival(some_asked, ar_sem).wait()
+    arrival(some_asked, as_sem).wait()
+    asked_in[at.d] = asked[at.d]
+    group = 128 // slots
+    count = lax.broadcasted_iota(jnp.int32, (per, 128), 0)
+    most = asked_in[0, 1:2, :]
+    for g in range(n // group):
+        wanted = asked_in[g * group, 0:1, :]
+        for j in range(1, group):
+            wanted = jnp.maximum(wanted, asked_in[g * group + j, 0:1, :])
+        for j in range(group):
+            most = jnp.maximum(most, asked_in[g * group + j, 1:2, :])
+        match = (wanted == count).astype(f32).astype(bf16)
+        owners_o[:, pl.ds(g * 128, 128)] = match
+        rows_out[pl.ds(g * 128, 128), :] = tn(match, table[...]).astype(bf16)
+    fullest[0] = jnp.broadcast_to(most, fullest.shape[1:])
+    to_beside(fullest.at[0], fullest.at[1], 7).start()
+
+    def slot_rows(ref, d):
+        return ref.at[pl.ds(multiple(d * slots, 16), slots)]
+
+    for d in others:
+        remote(slot_rows(rows_out, d), slot_rows(came, at.d), rs_sem, rr_sem, (at.s, d)).start()
+    gather.pass_z(u_wi)
+    gather.pass_z(u_wr)
+
+    @pl.when(is_decoder)
+    def _():
+        for own, _ in crossed[:1]:
+            gather.begin(own)
+
+    gather.begin(u_sq)
+
+    @pl.when(is_decoder)
+    def _():
+        arrival(crossed[0][1].src, x_recv.at[1]).wait()
+        gather.begin(crossed[0][1])
+        for k, (own, far) in enumerate(crossed[1:]):
+            gather.begin(own)
+            arrival(far.src, x_recv.at[2 + k]).wait()
+            gather.begin(far)
+
+    @pl.when(jnp.logical_not(is_decoder))
+    def _():
+        gather.begin(own_sm)
+        arrival(far_sm.src, x_recv.at[0]).wait()
+        gather.begin(far_sm)
+
+    gather.pass_y(u_wi)
+    some_rows = came.at[pl.ds(0, (n - 1) * slots)]
+    arrival(some_rows, rr_sem).wait()
+    arrival(some_rows, rs_sem).wait()
+    came[pl.ds(multiple(at.d * slots, 16), slots), :] = rows_out[
+        pl.ds(multiple(at.d * slots, 16), slots), :
+    ]
+    emb_o[...] = nn(hit[...], came[...]).astype(bf16)
+    to_beside(fullest.at[0], fullest.at[1], 7).wait()
+    most_o[...] = jnp.maximum(fullest[0], fullest[1])
+    for copy in locals_:
+        copy.wait()
+    gather.end(u_wi)
+
+    def input_drive(i, _):
+        cols = pl.ds(multiple(i * 512, 512), 512)
+        drive[:, cols] = nt(emb_o[...], wi[cols, :])
+        return _
+
+    lax.fori_loop(0, 3 * H // 512, input_drive, 0)
+    gather.pass_y(u_wr)
+    gather.end(u_wr)
+
+    def scan(ctx, service):
+        def step(t, h):
+            rows = pl.ds(multiple(t * R, R), R)
+            p = h * keep[rows, :]
+            rec[4, rows, :] = p
+            mix = nn(p.astype(bf16), wr[...])
+            d = drive[rows, :]
+            z_in = d[:, :H] + mix[:, :H]
+            r_in = d[:, H : 2 * H] + mix[:, H : 2 * H]
+            m = mix[:, 2 * H :]
+            if ctx is not None:
+                z_in += ctx[:, :H]
+                r_in += ctx[:, H : 2 * H]
+                m += ctx[:, 2 * H :]
+            z = jax.nn.sigmoid(z_in)
+            r = jax.nn.sigmoid(r_in)
+            cand = jnp.tanh(d[:, 2 * H :] + r * m)
+            h = z * p + (1.0 - z) * cand
+            rec[0, rows, :] = z
+            rec[1, rows, :] = r
+            rec[2, rows, :] = cand
+            rec[3, rows, :] = m
+            h_o[rows, :] = h.astype(bf16)
+            for when, what in service:
+                pl.when(t == when)(what)
+            return h
+
+        return lax.fori_loop(0, steps, step, jnp.zeros((R, H), f32))
+
+    def keep_copies(pairs):
+        copies = [pltpu.make_async_copy(a, b, o_sem.at[k]) for k, (a, b) in enumerate(pairs)]
+        for copy in copies:
+            copy.start()
+        return copies
+
+    last = pl.ds((steps - 1) * R, R)
+
+    @pl.when(jnp.logical_not(is_decoder))
+    def _():
+        copies = keep_copies([(wr, wr_o), (wi, wi_o)])
+        scan(None, [(2, lambda: gather.pass_z(u_sq)), (7, lambda: gather.pass_y(u_sq))])
+        gather.end(u_sq)
+        ctx_tanh = jnp.tanh(nn(h_o[last, :], sq[...]))
+        tanh_o[...] = ctx_tanh
+        ctx_o[...] = ctx_tanh.astype(bf16)
+        send = to_beside(ctx_o, ctx_o, 4)
+        send.start()
+        copies += [
+            pltpu.make_async_copy(rec, rec_o, o_sem.at[2]),
+            pltpu.make_async_copy(sq, sq_o, o_sem.at[3]),
+        ]
+        for copy in copies[2:]:
+            copy.start()
+        for u in (own_sm, far_sm):
+            gather.pass_z(u)
+        for u in (own_sm, far_sm):
+            gather.pass_y(u)
+        for u in (own_sm, far_sm):
+            gather.end(u)
+        send.wait_send()
+        for k, (src, dst) in enumerate([(cg_s, cg), (de_s, de), (dc_s, dc)]):
+            to_beside(src, block_rows(dst, 0, src.shape[0]), 1 + k).wait_send()
+
+        arrival(smooth_in, x_recv.at[5]).wait()
+        tile = 512
+        lanes = lax.broadcasted_iota(jnp.int32, (tokens, 128), 1)
+        m_part[...] = jnp.full(m_part.shape, -jnp.inf, f32)
+        s_part[...] = jnp.zeros_like(s_part)
+        p_part[...] = jnp.zeros_like(p_part)
+
+        def tops(i, _):
+            rows = pl.ds(multiple(i * tile, tile), tile)
+            logits = nt(smooth_in[...], sm[rows, :])
+            parts = [logits[:, k * 128 : (k + 1) * 128] for k in range(tile // 128)]
+            before = m_part[...]
+            top = before
+            for part in parts:
+                top = jnp.maximum(top, part)
+            total = s_part[...] * jnp.exp(before - top)
+            picked = p_part[...]
+            for k, part in enumerate(parts):
+                total += jnp.exp(part - top)
+                picked += jnp.where(lanes == labels[...] - (i * tile + k * 128), part, 0.0)
+            m_part[...] = top
+            s_part[...] = total
+            p_part[...] = picked
+            return _
+
+        lax.fori_loop(0, 2 * n * words // tile, tops, 0)
+        top = jnp.max(m_part[...], axis=1, keepdims=True)
+        total = jnp.sum(s_part[...] * jnp.exp(m_part[...] - top), axis=1, keepdims=True)
+        log_norm = top + jnp.log(total)
+        picked = jnp.sum(p_part[...], axis=1, keepdims=True)
+        scale = 1.0 / (R * n)
+        loss = jnp.sum(log_norm - picked, axis=0, keepdims=True) * scale
+        loss_o[...] = jnp.broadcast_to(loss, loss_o.shape)
+        m_part[...] = jnp.broadcast_to(log_norm, m_part.shape)
+        drive[:, pl.ds(0, M)] = jnp.zeros((tokens, M), f32)
+
+        def grads(i, _):
+            rows = pl.ds(multiple(i * tile, tile), tile)
+            weight = sm[rows, :]
+            logits = nt(smooth_in[...], weight)
+            low = []
+            for k in range(tile // 128):
+                part = jnp.exp(logits[:, k * 128 : (k + 1) * 128] - m_part[...])
+                hits = lanes == labels[...] - (i * tile + k * 128)
+                low.append(((part - jnp.where(hits, 1.0, 0.0)) * scale).astype(bf16))
+            low = jnp.concatenate(low, axis=1)
+            drive[:, pl.ds(0, M)] += nn(low, weight)
+            sm[rows, :] = tn(low, smooth_in[...]).astype(bf16)
+            return _
+
+        lax.fori_loop(0, 2 * n * words // tile, grads, 0)
+        grad_out[...] = drive[:, pl.ds(0, M)].astype(bf16)
+        send = to_beside(grad_out, grad_o, 6)
+        send.start()
+        copy = pltpu.make_async_copy(sm, term_o, o_sem.at[4])
+        copy.start()
+        copies.append(copy)
+        send.wait_send()
+        for copy in copies:
+            copy.wait()
+
+    @pl.when(is_decoder)
+    def _():
+        copies = keep_copies([(wr, wr_o), (wi, wi_o)])
+        cg_own, cg_far = crossed[0]
+        gather.pass_z(cg_own)
+        gather.pass_z(cg_far)
+        gather.pass_y(cg_own)
+        gather.pass_y(cg_far)
+        gather.pass_z(u_sq)
+        gather.end(cg_own)
+        gather.end(cg_far)
+        copies.append(pltpu.make_async_copy(cg, cg_o, o_sem.at[2]))
+        copies[-1].start()
+        arrival(ctx_o, x_recv.at[4]).wait()
+        rest = [u for pair in crossed[1:] for u in pair]
+        service = [(2 + k, functools.partial(gather.pass_z, u)) for k, u in enumerate(rest)]
+        service += [
+            (5 + k, functools.partial(gather.pass_y, u)) for k, u in enumerate([u_sq] + rest)
+        ]
+        ctx = nn(ctx_o[...], cg[...])
+        scan(ctx, service)
+        for u in [u_sq] + rest:
+            gather.end(u)
+        later = [(rec, rec_o), (sq, sq_o), (de, de_o), (dc, dc_o)]
+        later = [
+            pltpu.make_async_copy(a, b, o_sem.at[3 + k]) for k, (a, b) in enumerate(later)
+        ]
+        for copy in later:
+            copy.start()
+        copies += later
+        pre = nn(h_o[...], sq[...]) + nt(emb_o[...], de[...])
+        outer = nn(ctx_o[...], dc[...])
+        pre = (pre.reshape(steps, R, 2 * M) + outer[None]).reshape(tokens, 2 * M)
+        pre_o[...] = pre
+        a, b = pre[:, :M], pre[:, M:]
+        high = jnp.maximum(a, b)
+        smooth = high + jnp.log(jnp.exp(a - high) + jnp.exp(b - high))
+        grad_out[...] = smooth.astype(bf16)
+        send = to_beside(grad_out, smooth_in, 5)
+        send.start()
+        send.wait_send()
+        to_beside(sm_s, block_rows(sm, n, words), 0).wait_send()
+        arrival(grad_o, x_recv.at[6]).wait()
+        for copy in copies:
+            copy.wait()
+
+
+def forward(n, sizes, asked, hit, table, keep, labels, shards):
+    R, H, E, M, slots, per, words = sizes
+    Z, Y = factors(n)
+    tokens = hit.shape[0]
+    shape = jax.ShapeDtypeStruct
+    dma = pltpu.SemaphoreType.DMA
+    units = 9
+    cg_rows, de_rows, dc_rows = H, 2 * M, H
+    return pl.pallas_call(
+        functools.partial(forward_kernel, n, sizes),
+        out_shape=[
+            shape((H, 3 * H), bf16),
+            shape((3 * H, E), bf16),
+            shape((H, H), bf16),
+            shape((cg_rows, 3 * H), bf16),
+            shape((de_rows, E), bf16),
+            shape((dc_rows, 2 * M), bf16),
+            shape((2 * n * words, M), bf16),
+            shape((5, tokens, H), f32),
+            shape((tokens, H), bf16),
+            shape((tokens, E), bf16),
+            shape((tokens, 2 * M), f32),
+            shape((tokens, M), bf16),
+            shape((R, H), f32),
+            shape((R, H), bf16),
+            shape((8, 128), f32),
+            shape((8, 128), jnp.int32),
+            shape((per, n * slots), bf16),
+        ],
+        in_specs=[VMEM] * 5 + [ANY] * 7,
+        out_specs=[ANY] * 8 + [VMEM] * 9,
+        scratch_shapes=[
+            pltpu.VMEM((n, 8, 128), jnp.int32),
+            pltpu.VMEM((n * slots, E), bf16),
+            pltpu.VMEM((n * slots, E), bf16),
+            pltpu.VMEM((H, 3 * H), bf16),
+            pltpu.VMEM((3 * H, E), bf16),
+            pltpu.VMEM((H, H), bf16),
+            pltpu.VMEM((2 * n * words, M), bf16),
+            pltpu.VMEM((cg_rows, 3 * H), bf16),
+            pltpu.VMEM((de_rows, E), bf16),
+            pltpu.VMEM((dc_rows, 2 * M), bf16),
+            pltpu.VMEM((tokens, 3 * H), f32),
+            pltpu.VMEM((5, tokens, H), f32),
+            pltpu.VMEM((tokens, M), bf16),
+            pltpu.VMEM((tokens, M), bf16),
+            pltpu.VMEM((tokens, 128), f32),
+            pltpu.VMEM((tokens, 128), f32),
+            pltpu.VMEM((tokens, 128), f32),
+            pltpu.VMEM((2, 8, 128), jnp.int32),
+            dma((units, max(Z - 1, 1))),
+            dma((units, max(Z * (Y - 1), 1))),
+            dma((units,)),
+            dma((units,)),
+            dma((7,)),
+            dma((7,)),
+            dma((8,)),
+            dma((8,)),
+            dma,
+            dma,
+            dma,
+            dma,
+        ],
+        compiler_params=pltpu.CompilerParams(
+            collective_id=2, has_side_effects=True, vmem_limit_bytes=VMEM_LIMIT
+        ),
+    )(asked, hit, table, keep, labels, *shards)
+
+
+def in_rounds(
     token_ids,
     resets,
     targets,
@@ -599,6 +1108,7 @@
             deep_blocks,
             loss_blocks,
         ],
+        1,
     )
     deep_halves = deep_sum.reshape((2,) + deep_embed.shape)
     both = lax.ppermute(
@@ -623,6 +1133,197 @@
         context_out,
         softmax_sum,
     )
+
+
+def in_one_round(
+    token_ids,
+    resets,
+    targets,
+    embedding,
+    input_gates,
+    recur_gates,
+    square,
+    context_gates,
+    deep_embed,
+    deep_context,
+    softmax_weight,
+):
+    n = lax.axis_size("dp")
+    s = lax.axis_index("section")
+    d = lax.axis_index("dp")
+    is_decoder = s == 1
+    micro, rows, steps = token_ids.shape[1:]
+    R = micro * rows
+    tokens = R * steps
+    H = square.shape[2]
+    E = embedding.shape[2]
+    M = softmax_weight.shape[1]
+    per = embedding.shape[1]
+    slots = 512 // n
+
+    def time_major(x):
+        return jnp.transpose(x.reshape(R, steps), (1, 0)).reshape(-1)
+
+    ids = time_major(token_ids[0])
+    keep = time_major(1 - resets[0]).astype(f32)[:, None]
+    labels = time_major(targets)
+
+    plan = request_slots(ids, n, per, slots)
+    asked, hit = round_maps(plan, 0, n, slots)
+    lane = jnp.arange(128, dtype=jnp.int32)
+    asked = jnp.tile(asked.reshape(n, slots), (1, 128 // slots))
+    asked = jnp.where(lane // slots == d % (128 // slots), asked, -1)
+    fullest = jnp.broadcast_to(jnp.max(plan[2]), (n, 1, 128))
+    asked = jnp.concatenate([asked[:, None], fullest, jnp.zeros((n, 6, 128), jnp.int32)], axis=1)
+
+    shards = [
+        recur_gates[0],
+        input_gates[0],
+        square[0],
+        softmax_weight,
+        context_gates,
+        deep_embed,
+        deep_context,
+    ]
+    sizes = (R, H, E, M, slots, per, softmax_weight.shape[0])
+    results = forward(n, sizes, asked, hit, embedding[0], keep, labels[:, None], shards)
+
+    def rest():
+        (
+            wr,
+            wi,
+            sq,
+            cg,
+            de,
+            dc,
+            softmax_term,
+            rec,
+            states_low,
+            emb,
+            deep_pre,
+            smooth_grad,
+            ctx_tanh,
+            context,
+            loss,
+            _,
+            owners,
+        ) = results
+        loss = jnp.where(is_decoder, 0.0, loss[0, 0])
+        record = [rec[k] for k in range(5)]
+        last_low = states_low[-R:]
+        smooth = jnp.logaddexp(deep_pre[:, :M], deep_pre[:, M:])
+        smooth_grad = smooth_grad.astype(f32)
+
+        deep_grad = jnp.concatenate(
+            [
+                smooth_grad * jnp.exp(deep_pre[:, :M] - smooth),
+                smooth_grad * jnp.exp(deep_pre[:, M:] - smooth),
+            ],
+            axis=1,
+        )
+        deep_low = deep_grad.astype(bf16)
+        outer_low = jnp.sum(deep_grad.reshape(steps, R, -1), axis=0).astype(bf16)
+        state_grad = nt(deep_low, sq)
+        dec_low, dec_cand, drive_sum = gru_backward(
+            state_grad, jnp.zeros((R, H), f32), keep, record, wr
+        )
+        drive_sum_low = drive_sum.astype(bf16)
+        context_grad = (nt(outer_low, dc) + nt(drive_sum_low, cg)).astype(bf16)
+        packed = lax.all_gather(jnp.concatenate([context, outer_low, drive_sum_low], axis=1), "dp", tiled=True)
+        packed_came = lax.ppermute(packed, "section", [(1, 0)])
+        packed = jnp.where(is_decoder, packed, packed_came)
+
+        context_back = lax.ppermute(context_grad, "section", [(1, 0)])
+        pre_low = (context_back.astype(f32) * (1.0 - ctx_tanh * ctx_tanh)).astype(bf16)
+        enc_low, enc_cand, _ = gru_backward(
+            jnp.zeros((tokens, H), f32), nt(pre_low, sq), keep, record, wr
+        )
+
+        def pick(of_encoder, of_decoder):
+            return jnp.where(is_decoder, of_decoder, of_encoder)
+
+        recur_low = pick(enc_low, dec_low)
+        cand_low = pick(enc_cand, dec_cand)
+        before_low = record[4].astype(bf16)
+        drive_low = jnp.concatenate([recur_low[:, : 2 * H], cand_low], axis=1)
+        recur_term = tn(before_low, recur_low).astype(bf16)
+        input_term = tn(drive_low, emb).astype(bf16)
+        deep_mask = jnp.where(is_decoder, deep_low, jnp.zeros_like(deep_low))
+        input_grad = nn(drive_low, wi) + jnp.where(is_decoder, nn(deep_low, de), 0.0)
+        rows_pad = jnp.zeros((tokens - R, H), bf16)
+        square_term = tn(
+            pick(jnp.concatenate([last_low, rows_pad]), states_low),
+            pick(jnp.concatenate([pre_low, rows_pad]), deep_low),
+        ).astype(bf16)
+        deep_term = tn(deep_mask, emb).astype(bf16)
+
+        input_grad_low = input_grad.astype(bf16)
+
+        table_grad = nn(owners, swap(tn(hit, input_grad_low).astype(bf16), n))
+
+        half = softmax_term.shape[0] // 2
+        square_sum, recur_sum, input_sum, soft_0, soft_1, deep_0, deep_1, loss_sum = scatter(
+            n,
+            [
+                square_term.reshape((n,) + square.shape[1:]),
+                recur_term.reshape((n,) + recur_gates.shape[1:]),
+                input_term.reshape((n,) + input_gates.shape[1:]),
+                softmax_term[:half].reshape((n,) + softmax_weight.shape),
+                softmax_term[half:].reshape((n,) + softmax_weight.shape),
+                deep_term[:M].reshape((n,) + deep_embed.shape),
+                deep_term[M:].reshape((n,) + deep_embed.shape),
+                jnp.broadcast_to(loss, (n, 8, 128)),
+            ],
+            3,
+        )
+        deep_far = lax.ppermute(deep_0, "section", [(1, 0)])
+        deep_out = jnp.where(is_decoder, deep_1, deep_far)
+        soft_far, loss_far = lax.ppermute((soft_1, loss_sum), "section", [(0, 1)])
+        softmax_sum = jnp.where(is_decoder, soft_far, soft_0)
+        loss_out = jnp.where(is_decoder, loss_far, loss_sum)[0, 0]
+
+        own = (s * n + d) * context_gates.shape[0]
+        context_own = lax.dynamic_slice(packed, (0, own), (packed.shape[0], context_gates.shape[0]))
+        gates_out = tn(context_own, packed[:, H + 2 * M :])
+        context_out = tn(context_own, packed[:, H : H + 2 * M])
+
+        return (
+            loss_out,
+            table_grad[None],
+            input_sum[None],
+            recur_sum[None],
+            square_sum[None],
+            gates_out,
+            deep_out,
+            context_out,
+            softmax_sum,
+        )
+
+    def again():
+        return in_rounds(
+            token_ids,
+            resets,
+            targets,
+            embedding,
+            input_gates,
+            recur_gates,
+            square,
+            context_gates,
+            deep_embed,
+            deep_context,
+            softmax_weight,
+        )
+
+    return lax.cond(results[15][0, 0] < slots, rest, again)
+
+
+def per_device(*args):
+    n = lax.axis_size("dp")
+    blocks = [args[k].shape[-2] for k in (4, 5, 6, 7, 8, 9, 10)]
+    aligned = all(rows % 16 == 0 for rows in blocks)
+    if aligned and n % 8 == 0 and n <= 32:
+        return in_one_round(*args)
+    return in_rounds(*args)
 
 
 def solution(mesh):

time: 826 us -> 629 us (0.76)
  waiting for transfers between devices: 193 us -> 59.6 us
  blocking collectives: 54.3 us -> 0 us
  matrix products: 58.3 us -> 38.1 us
  Pallas kernels: 417 us -> 427 us
    ppermute x7 -> x5, waiting for transfers between devices: 146 us -> 5.76 us  [the longest x2 5.75 us: rest(): soft_far, loss_far = lax.ppermute((soft_1, loss_sum), 'section', [(0, 1)])]
    pmax x1 -> x0, blocking collectives: 40.7 us -> none  [per_device(): rounds = lax.pmax(jnp.max(plan[2]) // slots + 1, ('section', 'dp'))]
    pallas_call x1, Pallas kernels: 136 us -> 158 us  [scatter(): pl.pallas_call(functools.partial(scatter_kernel, n, count), out_shape=[ja...]
    dot_general x9 -> x2, matrix products: 20.3 us -> 6.54 us  [nn(): return jnp.dot(a, b, preferred_element_type=f32)]
    all_to_all x1 -> x0, blocking collectives: 13.6 us -> none  [swap(): lax.all_to_all(x.reshape((n, -1) + shape[1:]), 'dp', 0, 0, tiled=False)]
    pallas_call x3 -> x1, Pallas kernels: 222 us -> 210 us  [forward(): pl.pallas_call(functools.partial(forward_kernel, n, sizes), out_shape=[sh...]
    dot_general x9 -> x7, matrix products: 25.7 us -> 19.4 us  [tn(): lax.dot_general(a, b, (((0,), (0,)), ((), ())), preferred_element_type=f32)]
  transfers between devices with their start and end apart: 10 -> 7, of which waited for: 6 -> 2; matrix products, arithmetic and copies ran while one was open for 7% -> 9% of each run, Pallas kernels for 41% -> 30%
where the time goes in v2:
time: 629 us; the launch traced here: 620 us
  Pallas kernels  427 us (68%)
  waiting for transfers between devices  59.6 us (9%)
  local copies, waits for them, and re-layouts  38.3 us (6%)
  matrix products  38.1 us (6%)
  starting transfers between devices  17.4 us (3%)
  between operations  16.4 us (3%)
  other arithmetic  16 us (3%)
  loops' own time  6.89 us (1%)
    pallas_call x1, Pallas kernels, forward(): pl.pallas_call(functools.partial(forward_kernel, n, sizes), out_shape=[sh...  210 us
    pallas_call x1, Pallas kernels, scatter(): pl.pallas_call(functools.partial(scatter_kernel, n, count), out_shape=[ja...  158 us
    pallas_call x2, Pallas kernels, gru_backward(): pl.pallas_call(backward_kernel, out_shape=[shape((tokens, 3 * H), bf16),...  59.4 us
    all_gather x1, waiting for transfers between devices, rest(): lax.all_gather(jnp.concatenate([context, outer_low, drive_sum_low], axis=...  53.8 us
    dot_general x7, matrix products, tn(): lax.dot_general(a, b, (((0,), (0,)), ((), ())), preferred_element_type=f32)  19.4 us
  transfers between devices with their start and end apart: 7, of which 2 were waited for; matrix products, arithmetic and copies ran while one was open for 9% of the time, Pallas kernels for 30%

profile of v2, /device:TPU:0, one launch (start us, length us, event | category | flops | bytes accessed | tf_op | source)
XLA Modules:
  0.0 619.8 jit_solution(2774957584971518937)
XLA Ops:
  7.3 0.9 reshape_squeeze.3
  13.1 0.8 copy.86.refs_3_
  14.7 0.9 broadcast_in_dim_reshape.6.refs_4_
  15.6 209.8 %shard_map.194 = (bf16[1024,3072]{1,0:T(8,128)(2,1)}, bf16[3072,620]{1,0:T(8,128)(2,1)}, bf16[1024,1024]{1,0:T(8,128)(2,1)}, bf16[1024,3072]{1,0:T(8,128)(2,1)},...) custom-call(s32[16,8,128]{2,1,0:T(8,128)} %add_add_fusion.refs_0_, ...), custom_call_target="tpu_custom_call" | custom-call | tf_op jit(solution)/shard_map/pallas_call | solution.py:877
  225.4 1.2 slice.106
  227.4 380.9 %conditional.1 = (f32[240,512]{1,0:T(8,128)}, f32[]{:T(128)}, f32[1,480,620]{2,1,0:T(8,128)S(1)}, f32[1,192,620]{2,1,0:T(8,128)S(1)}, f32[1,64,3072]{2,1,0:T(8,1...) conditional(s32[]{:T(128)} %bitcast.69, ...), branch_computations={%region_4.21_spmd, %region_21.23_spmd} | conditional | flops 16809499648 | bytes 388592992 | solution.py:1317
  232.5 2.3 convert_multiply_fusion.1
  235.1 1.6 copy-done.6
  236.7 3.2 slice_bitcast_fusion
  239.9 0.8 copy.88.keep
  240.7 3.7 fusion.92.sg
  245.1 29.7 %branch_1_fun.3 = (bf16[384,3072]{1,0:T(8,128)(2,1)}, bf16[384,1024]{1,0:T(8,128)(2,1)}, f32[32,3072]{1,0:T(8,128)}) custom-call(f32[384,1024]{1,0:T(8,128)} %fusion.92.sg, f32[32,1024]{1,0:T(8,128)} %broadcast_43_carry0.0.carry0, f32[384,1]{1,0:T(8,128)} %copy.88.keep, f32[384,1024]{1,0:T(8,128)} %get-tuple-element.389.z, ...), custom_call_target="tpu_custom_call" | custom-call | tf_op jit(solution)/shard_map/cond/branch_1_fun/pallas_call | solution.py:384
  274.8 1.0 convert_element_type.155
  276.7 2.3 fusion.91
  279.0 4.7 fusion.6
  283.8 1.3 collective-permute-start
  285.1 53.8 %all-gather.5.cloned.1.call-done = bf16[512,5120]{1,0:T(8,128)(2,1)} async-done(((bf16[32,5120]{1,0:T(8,128)(2,1)}), bf16[512,5120]{1,0:T(8,128)(2,1)}) %all-gather.5.cloned.1.call-update) | async-done | bytes 5242896 | tf_op jit(solution)/shard_map/cond/branch_1_fun/all_gather | solution.py:1232
  338.9 1.5 collective-permute-start.2
  340.4 5.5 fusion.84
  345.9 0.9 convolution_convert_fusion.3
  346.9 1.0 slice.88
  347.9 1.1 copy.83
  349.0 1.1 copy.84
  350.1 1.2 slice.101
  351.9 0.9 multiply_convert_fusion
  352.8 1.4 fusion.93.carry0
  354.2 1.3 broadcast_41_sg.0.sg
  355.6 29.7 %branch_1_fun.4 = (bf16[384,3072]{1,0:T(8,128)(2,1)}, bf16[384,1024]{1,0:T(8,128)(2,1)}, f32[32,3072]{1,0:T(8,128)}) custom-call(f32[384,1024]{1,0:T(8,128)} %broadcast_41_sg.0.sg, f32[32,1024]{1,0:T(8,128)} %fusion.93.carry0, f32[384,1]{1,0:T(8,128)} %copy.88.keep, f32[384,1024]{1,0:T(8,128)} %get-tuple-element.389.z, f32[384,1024]{1,0:T(8,128)} %get-tuple-element.388.r, ...), custom_call_target="tpu_custom_call" | custom-call | tf_op jit(solution)/shard_map/cond/branch_1_fun/pallas_call | solution.py:384
  385.2 1.9 broadcast_select_fusion.1
  387.3 1.1 copy-done.22
  389.2 0.9 copy-done.27
  390.1 4.1 convolution_convert_fusion.1
  394.2 6.0 copy.82
  400.2 6.0 fusion.2
  406.2 3.0 fusion.5
  409.3 1.1 copy.85
  410.4 3.8 all-to-all-start
  414.2 2.7 convolution_convert_fusion.2
  416.8 6.8 %convolution_convert_fusion = bf16[3072,1024]{0,1:T(8,128)(2,1)} fusion(bf16[384,3072]{1,0:T(8,128)(2,1)S(1)} %broadcast_select_fusion.1, f32[5,384,1024]{2,1,0:T(8,128)} %get-tuple-element.199), kind=kOutput, calls=%fused_computation | convolution fusion | flops 2419064832 | bytes 9437184 | tf_op jit(solution)/shard_map/cond/branch_1_fun/dot_general | solution.py:27
  424.3 157.9 %branch_1_fun.5 = (f32[64,1024]{1,0:T(8,128)}, f32[64,3072]{1,0:T(8,128)}, f32[192,620]{1,0:T(8,128)}, f32[240,512]{1,0:T(8,128)}, f32[240,512]{1,0:T(8,128)}, /...) custom-call(bf16[8,2,64,1024]{3,2,1,0:T(8,128)(2,1)} %bitcast.208, bf16[8,2,64,3072]{3,2,1,0:T(8,128)(2,1)} %bitcast.195, ...), custom_call_target="tpu_custom_call" | custom-call | tf_op jit(solution)/shard_map/cond/branch_1_fun/pallas_call | solution.py:297
  582.2 8.2 %collective-permute-start.4 = (f32[240,512]{1,0:T(8,128)}, f32[240,512]{1,0:T(8,128)S(1)}, u32[]{:S(2)}, u32[]{:S(2)}) collective-permute-start(f32[240,512]{1,0:T(8,128)} %get-tuple-element.223), channel_id=1, source_target_pairs={{0,16},{1,17},{2,18},{3,19},{4,20},{5,21},{6,22},{7,23},{8,24},{9,... | collective-permute-start | bytes 1474568 | tf_op jit(solution)/shard_map/cond/branch_1_fun/ppermute | solution.py:1281
  590.4 1.3 collective-permute-start.1
  591.7 1.3 collective-permute-start.3
  593.0 5.7 collective-permute-done.1
  600.0 1.9 broadcast_select_fusion.3
  602.4 3.0 broadcast_select_fusion
  605.5 1.5 fusion
  609.2 0.9 copy.128
  (108 shorter events, 13.6 us)
Async XLA Ops:
  7.2 220.1 %copy-start.47 = (s32[1,2,16,12]{2,1,3,0:T(2,128)S(1)}, s32[1,2,16,12]{2,1,3,0:T(2,128)}, u32[]{:S(2)}) copy-start(s32[1,2,16,12]{2,1,3,0:T(2,128)} %param.17) | copy-start | bytes 4612
  7.2 220.1 %copy-start.48 = (s32[1,2,16,12]{2,1,3,0:T(2,128)S(1)}, s32[1,2,16,12]{2,1,3,0:T(2,128)}, u32[]{:S(2)}) copy-start(s32[1,2,16,12]{2,1,3,0:T(2,128)} %param.18) | copy-start | bytes 4612
  7.2 220.1 %copy-start.49 = (s32[2,16,12]{1,0,2:T(2,128)S(1)}, s32[2,16,12]{1,0,2:T(2,128)}, u32[]{:S(2)}) copy-start(s32[2,16,12]{1,0,2:T(2,128)} %param.19) | copy-start | bytes 4612
  7.2 220.1 %copy-start.34 = (bf16[1,480,620]{2,1,0:T(8,128)(2,1)S(1)}, bf16[1,480,620]{2,1,0:T(8,128)(2,1)}, u32[]{:S(2)}) copy-start(bf16[1,480,620]{2,1,0:T(8,128)(2,1)} %param.20) | copy-start | bytes 1785604
  7.2 220.1 %copy-start.15 = (bf16[1,64,3072]{2,1,0:T(8,128)(2,1)S(1)}, bf16[1,64,3072]{2,1,0:T(8,128)(2,1)}, u32[]{:S(2)}) copy-start(bf16[1,64,3072]{2,1,0:T(8,128)(2,1)} %param.22) | copy-start | bytes 1179652
  7.2 220.1 %copy-start.18 = (bf16[1,192,620]{2,1,0:T(8,128)(2,1)S(1)}, bf16[1,192,620]{2,1,0:T(8,128)(2,1)}, u32[]{:S(2)}) copy-start(bf16[1,192,620]{2,1,0:T(8,128)(2,1)} %param.21) | copy-start | bytes 714244
  7.2 220.1 %copy-start.35 = (bf16[1,64,1024]{2,1,0:T(8,128)(2,1)S(1)}, bf16[1,64,1024]{2,1,0:T(8,128)(2,1)}, u32[]{:S(2)}) copy-start(bf16[1,64,1024]{2,1,0:T(8,128)(2,1)} %param.23) | copy-start | bytes 393220
  7.3 220.1 %copy-start.33 = (bf16[32,3072]{1,0:T(8,128)(2,1)S(1)}, bf16[32,3072]{1,0:T(8,128)(2,1)}, u32[]{:S(2)}) copy-start(bf16[32,3072]{1,0:T(8,128)(2,1)} %refs_9_.1) | copy-start | bytes 589828
  7.3 220.1 %copy-start.43 = (bf16[32,620]{1,0:T(8,128)(2,1)S(1)}, bf16[32,620]{1,0:T(8,128)(2,1)}, u32[]{:S(2)}) copy-start(bf16[32,620]{1,0:T(8,128)(2,1)} %refs_10_.1) | copy-start | bytes 119044
  7.3 220.1 %copy-start.41 = (bf16[32,1024]{1,0:T(8,128)(2,1)S(1)}, bf16[32,1024]{1,0:T(8,128)(2,1)}, u32[]{:S(2)}) copy-start(bf16[32,1024]{1,0:T(8,128)(2,1)} %refs_11_.1) | copy-start | bytes 196612
  7.3 220.1 %copy-start.19 = (bf16[240,512]{1,0:T(8,128)(2,1)S(1)}, bf16[240,512]{1,0:T(8,128)(2,1)}, u32[]{:S(2)}) copy-start(bf16[240,512]{1,0:T(8,128)(2,1)} %refs_8_.1) | copy-start | bytes 737284
  12.5 0.6 copy-start.50
  232.4 2.4 copy-start.13
  232.4 106.5 %all-gather.5.cloned.1.call-start = ((), (), s32[]{:S(2)}) async-start(), calls=%async_computation.9 | async-start | bytes 5570560 | tf_op jit(solution)/shard_map/cond/branch_1_fun/all_gather | solution.py:1232
  232.5 4.2 copy-start.6
  234.9 111.0 %copy-start.32 = (bf16[384,1024]{1,0:T(8,128)(2,1)}, bf16[384,1024]{1,0:T(8,128)(2,1)S(1)}, u32[]{:S(2)}) copy-start(bf16[384,1024]{1,0:T(8,128)(2,1)S(1)} %fusion.32) | copy-start | bytes 2359300 | tf_op jit(solution)/shard_map/cond
  236.7 3.2 copy-start.51
  245.1 30.8 %copy-start.46 = (bf16[32,1024]{1,0:T(8,128)(2,1)S(1)}, bf16[32,1024]{1,0:T(8,128)(2,1)}, u32[]{:S(2)}) copy-start(bf16[32,1024]{1,0:T(8,128)(2,1)} %get-tuple-element.219) | copy-start | bytes 196612 | tf_op jit(solution)/shard_map/cond
  283.8 68.1 %collective-permute-start = (bf16[32,1024]{1,0:T(8,128)(2,1)S(1)}, bf16[32,1024]{1,0:T(8,128)(2,1)}, u32[]{:S(2)}, u32[]{:S(2)}) collective-permute-start(bf16[32,1024]{1,0:T(8,128)(2,1)S(1)} %fusion.6), channel_id=1, source_target_pairs={{16,0},{17,1},{18,2},{19,3},{20,4},{21,5},{22,6},{23,7},{24,8},{25... | collective-permute-start | bytes 196616 | tf_op jit(solution)/shard_map/cond/branch_1_fun/ppermute | solution.py:1236
  338.9 263.5 %collective-permute-start.2 = (bf16[512,5120]{1,0:T(8,128)(2,1)}, bf16[512,5120]{1,0:T(8,128)(2,1)}, u32[]{:S(2)}, u32[]{:S(2)}) collective-permute-start(bf16[512,5120]{1,0:T(8,128)(2,1)} %all-gather.5.cloned.1.call-done), channel_id=1, source_target_pairs={{16,0},{17,1},{18,2},{19,3},{20,4},{21,5},{22,6},{23,7},{24,8},{25... | collective-permute-start | bytes 15728648 | tf_op jit(solution)/shard_map/cond/branch_1_fun/ppermute | solution.py:1233
  340.4 5.5 copy-start.54
  346.8 6.0 copy-start.10
  387.2 1.3 copy-start.22
  387.2 1.9 copy-start.24
  387.2 2.9 copy-start.55
  387.3 1.9 copy-start.12
  389.2 0.9 copy-start.27
  400.2 6.0 copy-start.14
  410.4 191.5 %all-to-all-start = ((bf16[16,32,620]{2,1,0:T(8,128)(2,1)}), bf16[16,32,620]{2,1,0:T(8,128)(2,1)S(1)}, u32[]{:S(2)}, u32[]{:S(2)}) async-start(bf16[16,32,620]{2,1,0:T(8,128)(2,1)} %bitcast.203), calls=%async_computation | async-start | bytes 1310720 | tf_op jit(solution)/shard_map/cond/branch_1_fun/all_to_all | solution.py:421
  424.3 177.6 %copy-start.36 = (bf16[480,512]{1,0:T(8,128)(2,1)S(1)}, bf16[480,512]{1,0:T(8,128)(2,1)}, u32[]{:S(2)}) copy-start(bf16[480,512]{1,0:T(8,128)(2,1)} %get-tuple-element.215) | copy-start | bytes 1474564 | tf_op jit(solution)/shard_map/cond
  582.2 17.8 %collective-permute-start.4 = (f32[240,512]{1,0:T(8,128)}, f32[240,512]{1,0:T(8,128)S(1)}, u32[]{:S(2)}, u32[]{:S(2)}) collective-permute-start(f32[240,512]{1,0:T(8,128)} %get-tuple-element.223), channel_id=1, source_target_pairs={{0,16},{1,17},{2,18},{3,19},{4,20},{5,21},{6,22},{7,23},{8,24},{9,... | collective-permute-start | bytes 1474568 | tf_op jit(solution)/shard_map/cond/branch_1_fun/ppermute | solution.py:1281
  590.4 8.4 %collective-permute-start.1 = (f32[8,128]{1,0:T(8,128)}, f32[8,128]{1,0:T(8,128)S(1)}, u32[]{:S(2)}, u32[]{:S(2)}) collective-permute-start(f32[8,128]{1,0:T(8,128)} %get-tuple-element.211), channel_id=1, source_target_pairs={{0,16},{1,17},{2,18},{3,19},{4,20},{5,21},{6,22},{7,23},{8,24},{9,... | collective-permute-start | bytes 12296 | tf_op jit(solution)/shard_map/cond/branch_1_fun/ppermute | solution.py:1281
  591.7 8.3 %collective-permute-start.3 = (f32[32,620]{1,0:T(8,128)}, f32[32,620]{1,0:T(8,128)S(1)}, u32[]{:S(2)}, u32[]{:S(2)}) collective-permute-start(f32[32,620]{1,0:T(8,128)} %get-tuple-element.222), channel_id=1, source_target_pairs={{16,0},{17,1},{18,2},{19,3},{20,4},{21,5},{22,6},{23,7},{24,8},{25... | collective-permute-start | bytes 238088 | tf_op jit(solution)/shard_map/cond/branch_1_fun/ppermute | solution.py:1279
  605.5 1.9 copy-start.28
  605.5 1.9 copy-start.37
  608.3 3.2 copy-start
  608.4 3.2 copy-start.44
  608.4 3.2 copy-start.45
  608.4 1.7 copy-start.42
  608.4 2.4 copy-start.38
Sparse Core Ops, SparseCore 0:
  276.8 62.0 all-gather.4
